TPU v7x, 32 devices: a whole 2x2x4 slice. The times are simulated.
32 devices in a mesh: seq: 8 (over y, x, core), dp: 4 (over z).
Axes of the slice: x: 2, y: 2, z: 4, core: 2. Of those that a mesh axis runs over, the one named last changes fastest.
Arguments:
- inputs: bfloat16 [16, 1024, 768], P('dp', 'seq'), may hold values from -6 to 6
- cotangent: bfloat16 [16, 1024, 768], P('dp', 'seq'), may hold values from -6 to 6
- neighbours: bfloat16 [16, 16, 2, 128, 768], P('dp', 'seq'), may hold values from -6 to 6
- presence: int32 [16, 16, 2], P('dp', 'seq'), may hold values 0 or 1
- row_order: int32 [768], replicated, may hold values from 0 to 767, each once
- w_master: float32 [768, 12288], P('dp', 'seq')
- w_first: float32 [768, 12288], P('dp', 'seq'), may hold values from -80 to 80
- w_second: float32 [768, 12288], P('dp', 'seq'), may hold values from 819.2 to 3276.8
- w_average: float32 [768, 12288], P('dp', 'seq'), may hold values from -0.21875 to 0.21875
- n_master: float32 [6, 768], P(None, 'dp')
- n_first: float32 [6, 768], P(None, 'dp'), may hold values from -80 to 80
- n_second: float32 [6, 768], P(None, 'dp'), may hold values from 819.2 to 3276.8
- n_average: float32 [6, 768], P(None, 'dp'), may hold values from 0.5 to 1.5
Outputs:
- outputs: bfloat16 [16, 1024, 768], P('dp', 'seq')
- grad_inputs: float32 [16, 1024, 768], P('dp', 'seq')
- w_first_new: float32 [768, 12288], P('dp', 'seq')
- w_second_new: float32 [768, 12288], P('dp', 'seq')
- w_new: float32 [768, 12288], P('dp', 'seq')
- w_average_new: float32 [768, 12288], P('dp', 'seq')
- n_first_new: float32 [6, 768], P(None, 'dp')
- n_second_new: float32 [6, 768], P(None, 'dp')
- n_new: float32 [6, 768], P(None, 'dp')
- n_average_new: float32 [6, 768], P(None, 'dp')
Inputs may be any that keep to these rules, and one draw needn't show every extreme that they name: A permutation of the weight rows: state row j holds weight row row_order[j]. `presence`: 1 where the neighbour exists; a span may have none.
All inputs are finite; a program needn't handle non-finite values. No bound on the sum of `presence` on one device may be relied on, other than what follows from the above.
Results may differ from a plain program's by a relative error of at most 0.025.
Values may be sent and summed in bfloat16 or wider, within the bound.
A program may use at most 320 MiB of HBM per device.

v0:
```python
from functools import partial

import jax
import jax.numpy as jnp
from jax import lax
from jax.experimental import pallas as pl
from jax.experimental.pallas import tpu as pltpu
from jax.sharding import PartitionSpec as P

HEAD = 64
STEP = 5
LANES = 128
SCALE = HEAD ** (-0.5)

beta_first = 0.9
beta_second = 0.95
adam_eps = 1e-08
learn_rate = 0.04
norm_rate = 0.6
weight_decay = 0.1
ema_decay = 0.5
norm_eps = 1e-05
masked_score = -1e30
VMEM_BYTES = 60 * 1024 * 1024
bf16 = jnp.bfloat16
f32 = jnp.float32


def mm(left, right):
    return lax.dot_general(left, right, (((1,), (0,)), ((), ())), preferred_element_type=f32)


def nt(left, right):
    return lax.dot_general(left, right, (((1,), (1,)), ((), ())), preferred_element_type=f32)


def tn(left, right):
    return lax.dot_general(left, right, (((0,), (0,)), ((), ())), preferred_element_type=f32)


def params():
    return pltpu.CompilerParams(vmem_limit_bytes=VMEM_BYTES)


def rows_of(index, size):
    return pl.ds(pl.multiple_of(index * size, size), size)


def centre_scale(values):
    centre = jnp.mean(values, axis=-1, keepdims=True)
    centred = values - centre
    spread = jnp.mean(centred * centred, axis=-1, keepdims=True)
    recip = lax.rsqrt(spread + norm_eps)
    return centred * recip, recip


def norm_back(upstream, normed, recip, gain):
    scaled = upstream * gain
    inner = (
        scaled
        - jnp.mean(scaled, axis=-1, keepdims=True)
        - normed * jnp.mean(scaled * normed, axis=-1, keepdims=True)
    )
    return (
        recip * inner,
        jnp.sum(upstream * normed, axis=0, keepdims=True),
        jnp.sum(upstream, axis=0, keepdims=True),
    )


def gelu_parts(value):
    const = 0.7978845608028654
    square = value * value
    bend = jnp.tanh(const * value * (1.0 + 0.044715 * square))
    half = 0.5 * (1.0 + bend)
    slope = half + 0.5 * value * (1.0 - bend * bend) * (const * (1.0 + 3 * 0.044715 * square))
    return value * half, slope


def head_mask(rows, half):
    lane = lax.broadcasted_iota(jnp.int32, (rows, LANES), 1)
    return (lane < HEAD) if half == 0 else (lane >= HEAD)


def pick(mask, value):
    return jnp.where(mask, value, jnp.zeros_like(value))


MESH = pl.DeviceIdType.MESH


class Place:
    def __init__(self, lines):
        self.lines = lines
        self.z = lax.axis_index("dp")
        self.me = lax.axis_index("seq")
        core, x, y = self.me % 2, (self.me // 2) % 2, self.me // 4
        self.core, self.x, self.y, self.chip = core, x, y, self.me // 2
        self.sib = self.me + 1 - 2 * core
        self.xn = self.me + 2 - 4 * x
        self.yn = self.me + 4 - 8 * y
        self.dg = self.xn + 4 - 8 * y

    def events(self):
        found = [(None, self.z, 0, 0)]
        for far in range(1, self.lines):
            found.append((self.z >= far, self.z - far, far, -1))
            found.append((self.z + far < self.lines, self.z + far, far, 1))
        return found

    def plane(self):
        return [lax.rem(self.me + step, 8) for step in range(1, 8)]

    def line(self):
        return [lax.rem(self.z + step, self.lines) for step in range(1, self.lines)]

    def meet(self):
        barrier = pltpu.get_barrier_semaphore()
        for other in self.plane():
            pl.semaphore_signal(
                barrier, inc=1, device_id={"dp": self.z, "seq": other}, device_id_type=MESH
            )
        for other in self.line():
            pl.semaphore_signal(
                barrier, inc=1, device_id={"dp": other, "seq": self.me}, device_id_type=MESH
            )
        pl.semaphore_wait(barrier, 7 + self.lines - 1)


def when(condition, body):
    if condition is None:
        body()
    else:
        pl.when(condition)(body)


def both(first, second):
    if first is None or second is None:
        return second if first is None else first
    return jnp.logical_and(first, second)


class Sender:
    def __init__(self, place, send_sems):
        self.place, self.sems, self.open = place, send_sems, []

    def start(self, condition, src, dst, recv_sem, z=None, seq=None):
        place = self.place
        target = {"dp": place.z if z is None else z, "seq": place.me if seq is None else seq}
        copy = pltpu.make_async_remote_copy(
            src_ref=src,
            dst_ref=dst,
            send_sem=self.sems.at[len(self.open)],
            recv_sem=recv_sem,
            device_id=target,
            device_id_type=MESH,
        )
        self.open.append((condition, copy))
        when(condition, copy.start)

    def arrived(self, condition, ref, recv_sem):
        copy = pltpu.make_async_remote_copy(
            src_ref=ref,
            dst_ref=ref,
            send_sem=self.sems.at[0],
            recv_sem=recv_sem,
            device_id={"dp": self.place.z, "seq": self.place.sib},
            device_id_type=MESH,
        )
        when(condition, copy.wait_recv)

    def finish(self):
        for condition, copy in self.open:
            when(condition, copy.wait_send)


class Weave:
    def __init__(self, steps):
        self.steps = list(steps)

    def some(self, count):
        for _ in range(min(count, len(self.steps))):
            self.steps.pop(0)()

    def rest(self):
        self.some(len(self.steps))


def unit_of(ref, lines, line, seq, begin=0, size=None):
    rows, cols = ref.shape[0] // lines, ref.shape[1] // 8
    size = rows if size is None else size
    return ref.at[
        pl.ds(pl.multiple_of(line * rows + begin, 16), size),
        pl.ds(pl.multiple_of(seq * cols, cols), cols),
    ]


def weight_copies(pairs, dim, wts_ref, w_ref, sems):
    width = pairs * LANES
    first = lax.rem(lax.axis_index("seq"), dim // width) * width
    return [
        pltpu.make_async_copy(
            wts_ref.at[:, pl.ds(pl.multiple_of(first + part * dim, LANES), width)],
            w_ref.at[:, pl.ds(part * width, width)],
            sems.at[part],
        )
        for part in range(3)
    ]


def pair_forward(pair, pairs, qkv_ref, att_ref, lse_ref, between):
    length = att_ref.shape[0]
    tile = 256
    below = lax.broadcasted_iota(jnp.int32, (tile, tile), 1) <= lax.broadcasted_iota(
        jnp.int32, (tile, tile), 0
    )
    masks = [head_mask(tile, 0), head_mask(tile, 1)]
    lane = lax.broadcasted_iota(jnp.int32, (tile, LANES), 1)
    for step in range(length // tile):
        rows = slice(step * tile, (step + 1) * tile)
        query = qkv_ref[pair, rows, :] * SCALE
        keys_here = qkv_ref[pairs + pair, rows, :]
        values_here = qkv_ref[2 * pairs + pair, rows, :]
        outs, logs = [], []
        for half in range(2):
            mine = pick(masks[half], query)
            here = jnp.where(below, nt(mine, keys_here), masked_score)
            peak = jnp.max(here, axis=-1, keepdims=True)
            if step:
                past = nt(mine, qkv_ref[pairs + pair, : step * tile, :])
                peak = jnp.maximum(peak, jnp.max(past, axis=-1, keepdims=True))
                past = jnp.exp(past - peak)
            here = jnp.exp(here - peak)
            total = jnp.sum(here, axis=-1, keepdims=True)
            out = mm(here.astype(bf16), values_here)
            if step:
                total = total + jnp.sum(past, axis=-1, keepdims=True)
                out = out + mm(past.astype(bf16), qkv_ref[2 * pairs + pair, : step * tile, :])
            outs.append(out / total)
            logs.append(peak + jnp.log(total))
        lse_ref[pair, :, rows] = jnp.where(lane == 0, logs[0], logs[1]).T[0:2, :]
        att_ref[rows, pl.ds(pl.multiple_of(pair * LANES, LANES), LANES)] = jnp.where(
            masks[0], outs[0], outs[1]
        ).astype(bf16)
        between()


def norm_rows(x_ref, norms, perm_ref, hid_ref):
    tile = 256

    @pl.loop(0, x_ref.shape[0] // tile)
    def _(step):
        rows = rows_of(step, tile)
        normed, _ = centre_scale(x_ref[rows, :].astype(f32))
        hidden = (normed * norms[0:1, :] + norms[1:2, :]).astype(bf16)
        hid_ref[rows, :] = mm(hidden, perm_ref[...]).astype(bf16)


def triple_part(part, pairs, hid_ref, w_ref, qkv_ref):
    width = pairs * LANES
    triple = mm(hid_ref[...], w_ref[:, part * width : (part + 1) * width]).astype(bf16)
    for pair in range(pairs):
        qkv_ref[part * pairs + pair] = triple[:, pair * LANES : (pair + 1) * LANES]


def self_forward_kernel(
    pairs, x_ref, norms_ref, perm_ref, w_ref, hid_ref, qkv_ref, att_ref, lse_ref
):
    norm_rows(x_ref, norms_ref, perm_ref, hid_ref)
    for part in range(3):
        triple_part(part, pairs, hid_ref, w_ref, qkv_ref)

    @pl.loop(0, pairs)
    def _(pair):
        pair_forward(pair, pairs, qkv_ref, att_ref, lse_ref, lambda: None)


def self_forward(pairs, x, norms, perm, w):
    length, dim = x.shape
    return pl.pallas_call(
        partial(self_forward_kernel, pairs),
        out_shape=(
            jax.ShapeDtypeStruct((length, dim), bf16),
            jax.ShapeDtypeStruct((3 * pairs, length, LANES), bf16),
            jax.ShapeDtypeStruct((length, pairs * LANES), bf16),
            jax.ShapeDtypeStruct((pairs, 2, length), f32),
        ),
        compiler_params=params(),
        name="self_forward",
    )(x, norms, perm, w)


def pair_backward(pair, pairs, qkv_ref, att_ref, gatt_ref, lse_ref, grad_ref, acc_ref, between):
    length = att_ref.shape[0]
    width = pairs * LANES
    tile = 256
    above = lax.broadcasted_iota(jnp.int32, (tile, tile), 0) <= lax.broadcasted_iota(
        jnp.int32, (tile, tile), 1
    )
    masks = [head_mask(tile, 0), head_mask(tile, 1)]
    lanes = pl.ds(pl.multiple_of(pair * LANES, LANES), LANES)
    for step in range(length // tile):
        rows = slice(step * tile, (step + 1) * tile)
        query = qkv_ref[pair, rows, :] * SCALE
        grad_out = gatt_ref[rows, lanes]
        product = grad_out.astype(f32) * att_ref[rows, lanes].astype(f32)
        queries = [pick(masks[half], query) for half in range(2)]
        grads = [pick(masks[half], grad_out) for half in range(2)]
        deltas = [jnp.sum(pick(masks[half], product).T, axis=0, keepdims=True) for half in range(2)]
        grad_query = [None, None]
        for other in range(step + 1):
            cols = slice(other * tile, (other + 1) * tile)
            keys = qkv_ref[pairs + pair, cols, :]
            values = qkv_ref[2 * pairs + pair, cols, :]
            key_part = value_part = None
            for half in range(2):
                scores = nt(keys, queries[half])
                if other == step:
                    scores = jnp.where(above, scores, masked_score)
                probs = jnp.exp(scores - lse_ref[pair, half : half + 1, rows])
                grad_scores = (probs * (nt(values, grads[half]) - deltas[half])).astype(bf16)
                query_term = tn(grad_scores, keys)
                grad_query[half] = (
                    query_term if grad_query[half] is None else grad_query[half] + query_term
                )
                key_term = mm(grad_scores, queries[half])
                value_term = mm(probs.astype(bf16), grads[half])
                key_part = key_term if key_part is None else key_part + key_term
                value_part = value_term if value_part is None else value_part + value_term
            if other == step:
                acc_ref[0, cols, :] = key_part
                acc_ref[1, cols, :] = value_part
            else:
                acc_ref[0, cols, :] += key_part
                acc_ref[1, cols, :] += value_part
        grad_ref[rows, lanes] = (jnp.where(masks[0], grad_query[0], grad_query[1]) * SCALE).astype(
            bf16
        )
        between()
    for part in range(2):
        lanes_to = pl.ds(pl.multiple_of((part + 1) * width + pair * LANES, LANES), LANES)
        grad_ref[:, lanes_to] = acc_ref[part].astype(bf16)


def self_backward_kernel(
    pairs,
    qkv_ref,
    att_ref,
    gatt_ref,
    lse_ref,
    hid_ref,
    w_ref,
    gw_ref,
    ghid_ref,
    grad_ref,
    acc_ref,
):
    length = att_ref.shape[0]
    width = pairs * LANES
    attention = (qkv_ref, att_ref, gatt_ref, lse_ref, grad_ref, acc_ref)

    @pl.loop(0, pairs)
    def _(pair):
        pair_backward(pair, pairs, *attention, lambda: None)

    hidden_t = hid_ref[...].T
    for part in range(3):
        cols = slice(part * width, (part + 1) * width)
        gw_ref[:, cols] = mm(hidden_t, grad_ref[:, cols]).astype(bf16)
    for begin in range(0, length, 256):
        rows = slice(begin, begin + 256)
        ghid_ref[rows, :] = nt(grad_ref[rows, :], w_ref[...]).astype(bf16)


def self_backward(pairs, qkv, att, gatt, lse, hid, w):
    length, dim = hid.shape
    width = pairs * LANES
    return pl.pallas_call(
        partial(self_backward_kernel, pairs),
        out_shape=(
            jax.ShapeDtypeStruct((dim, 3 * width), bf16),
            jax.ShapeDtypeStruct((length, dim), bf16),
        ),
        scratch_shapes=[
            pltpu.VMEM((length, 3 * width), bf16),
            pltpu.VMEM((2, length, LANES), f32),
        ],
        compiler_params=params(),
        name="self_backward",
    )(qkv, att, gatt, lse, hid, w)


def finish_kernel(
    pairs,
    lines,
    qkv_ref,
    att_ref,
    gatt_ref,
    lse_ref,
    hid_ref,
    x_ref,
    gfirst_ref,
    norms_ref,
    perm_ref,
    others_ref,
    wts_ref,
    _,
    all_ref,
    gin_ref,
    small_ref,
    grad_ref,
    acc_ref,
    gw_ref,
    w_ref,
    sems,
    ghid_ref,
    gsib_ref,
    parts_ref,
    gsib_sems,
    part_sems,
    send_sems,
):
    length, dim = hid_ref.shape
    width = pairs * LANES
    tokens = length // 8
    place = Place(lines)
    me, core = place.me, place.core
    place.meet()
    send = Sender(place, send_sems)
    copies = weight_copies(pairs, dim, wts_ref, w_ref, sems)
    for copy in copies:
        copy.start()

    share_count = dim // width
    share = lax.rem(me, share_count)
    gw_ref[3] = jnp.zeros_like(gw_ref[3])
    outs = []
    for part in range(3):
        for other in range(1, share_count):
            first = part * dim + lax.rem(share + other, share_count) * width
            outs.append(
                pltpu.make_async_copy(
                    gw_ref.at[3],
                    all_ref.at[:, pl.ds(pl.multiple_of(first, LANES), width)],
                    sems.at[6 + part * (share_count - 1) + other - 1],
                )
            )
            outs[-1].start()

    attention = (qkv_ref, att_ref, gatt_ref, lse_ref, grad_ref, acc_ref)

    @pl.loop(0, pairs)
    def _(pair):
        pair_backward(pair, pairs, *attention, lambda: None)

    def token_rows(device):
        return pl.ds(pl.multiple_of(device * tokens, tokens), tokens)

    for copy in copies:
        copy.wait()
    for begin in range(0, length, 256):
        rows = slice(begin, begin + 256)
        ghid_ref[rows, :] = nt(grad_ref[rows, :], w_ref[...]).astype(bf16)
    chips = (place.xn // 2, place.yn // 2, place.dg // 2, place.chip)
    for chip in chips:
        theirs = chip * 2 + 1 - core
        send.start(
            None, ghid_ref.at[token_rows(theirs)], gsib_ref.at[chip], gsib_sems.at[chip], seq=place.sib
        )
    for chip in chips:
        send.arrived(None, gsib_ref.at[chip], gsib_sems.at[chip])
        rows = token_rows(chip * 2 + core)
        total = (ghid_ref[rows, :].astype(f32) + gsib_ref[chip].astype(f32)).astype(bf16)
        if chip is place.chip:
            parts_ref[chip] = total
        else:
            ghid_ref[rows, :] = total
            send.start(
                None,
                ghid_ref.at[rows],
                parts_ref.at[place.chip],
                part_sems.at[place.chip],
                seq=chip * 2 + core,
            )

    hidden_t = hid_ref[...].T
    for part in range(3):
        gw_ref[part] = mm(hidden_t, grad_ref[:, part * width : (part + 1) * width]).astype(bf16)
        first = part * dim + share * width
        outs.append(
            pltpu.make_async_copy(
                gw_ref.at[part],
                all_ref.at[:, pl.ds(pl.multiple_of(first, LANES), width)],
                sems.at[3 + part],
            )
        )
        outs[-1].start()

    for chip in chips[:3]:
        send.arrived(None, parts_ref.at[chip], part_sems.at[chip])
    gain_sum = shift_sum = None
    for chip in range(4):
        rows = slice(chip * tokens, (chip + 1) * tokens)
        upstream = nt(parts_ref[chip], perm_ref[...])
        normed, recip = centre_scale(x_ref[rows, :].astype(f32))
        back, gain, shift = norm_back(upstream, normed, recip, norms_ref[0:1, :])
        gin_ref[rows, :] = gfirst_ref[rows, :] + back
        gain_sum = gain if gain_sum is None else gain_sum + gain
        shift_sum = shift if shift_sum is None else shift_sum + shift
    small_ref[...] = others_ref[...]
    small_ref[0:1, :] = gain_sum
    small_ref[1:2, :] = shift_sum
    for copy in outs:
        copy.wait()
    send.finish()


def finish(pairs, lines, qkv, att, gatt, lse, hid, x, gfirst, norms, perm, others, weights, grads):
    length, dim = hid.shape
    width = pairs * LANES
    count = x.shape[0]
    tokens = length // 8
    any_space = pl.BlockSpec(memory_space=pl.ANY)
    vmem = pl.BlockSpec(memory_space=pltpu.VMEM)
    dma = pltpu.SemaphoreType.DMA
    return pl.pallas_call(
        partial(finish_kernel, pairs, lines),
        out_shape=(
            jax.ShapeDtypeStruct(grads.shape, bf16),
            jax.ShapeDtypeStruct((count, dim), f32),
            jax.ShapeDtypeStruct((8, dim), f32),
        ),
        in_specs=[vmem] * 10 + [any_space] * 2,
        out_specs=(any_space, vmem, vmem),
        scratch_shapes=[
            pltpu.VMEM((length, 3 * width), bf16),
            pltpu.VMEM((2, length, LANES), f32),
            pltpu.VMEM((4, dim, width), bf16),
            pltpu.VMEM((dim, 3 * width), bf16),
            dma((6 + 3 * (dim // width),)),
            pltpu.VMEM((length, dim), bf16),
            pltpu.VMEM((4, tokens, dim), bf16),
            pltpu.VMEM((4, tokens, dim), bf16),
            dma((4,)),
            dma((4,)),
            dma((8,)),
        ],
        input_output_aliases={11: 0},
        compiler_params=pltpu.CompilerParams(
            vmem_limit_bytes=VMEM_BYTES, collective_id=3, has_side_effects=True
        ),
        name="finish",
    )(qkv, att, gatt, lse, hid, x, gfirst, norms, perm, others, weights, grads)


def spread_heads(block, rows, group):
    lane = lax.broadcasted_iota(jnp.int32, block.shape, 1) // HEAD
    return jnp.concatenate([pick(lane == head, block) for head in range(group)], axis=0)


def gather_heads(stacked, rows, group):
    lane = lax.broadcasted_iota(jnp.int32, (rows, stacked.shape[1]), 1) // HEAD
    out = None
    for head in range(group):
        part = pick(lane == head, stacked[head * rows : (head + 1) * rows])
        out = part if out is None else out + part
    return out


def live_keys(presence_ref, span, shape, axis, neighbours, each):
    index = lax.broadcasted_iota(jnp.int32, shape, axis) // each
    live = jnp.zeros(shape, f32)
    anyone = None
    for which in range(neighbours):
        here = presence_ref[span * neighbours + which]
        there = jnp.where(here > 0, 1.0, 0.0).astype(f32)
        live = jnp.where(index == which, there, live)
        anyone = here if anyone is None else jnp.maximum(anyone, here)
    return live, anyone.astype(f32)


def span_forward(span, spans, neighbours, presence_ref, cross_q_ref, near_kv_ref, cross_ref):
    count, dim = cross_q_ref.shape
    span_len = count // spans
    near = near_kv_ref.shape[0] // spans
    group = 256 // HEAD
    rows = rows_of(span, span_len)
    keys = rows_of(span, near)
    live, anyone = live_keys(presence_ref, span, (1, near), 1, neighbours, near // neighbours)
    for begin in range(0, dim, group * HEAD):
        lanes = slice(begin, begin + group * HEAD)
        lanes_v = slice(dim + begin, dim + begin + group * HEAD)
        query = spread_heads(cross_q_ref[rows, lanes] * SCALE, span_len, group)
        scores = jnp.where(live > 0, nt(query, near_kv_ref[keys, lanes]), masked_score)
        peak = jnp.max(scores, axis=-1, keepdims=True)
        expon = jnp.exp(scores - peak) * live
        total = jnp.sum(expon, axis=-1, keepdims=True) + 1.0 - anyone
        out = mm(expon.astype(bf16), near_kv_ref[keys, lanes_v]) / total
        cross_ref[rows, lanes] = gather_heads(out, span_len, group).astype(bf16)


def cross_forward_kernel(
    spans,
    neighbours,
    presence_ref,
    att_ref,
    x_ref,
    norms_ref,
    perm_ref,
    perm_att_ref,
    near_ref,
    w_out_ref,
    w_cq_ref,
    w_ck_ref,
    w_cv_ref,
    w_co_ref,
    att_p_ref,
    first_ref,
    hid_p_ref,
    cross_q_ref,
    near_p_ref,
    near_kv_ref,
    co_p_ref,
    second_ref,
    cross_ref,
):
    count, dim = x_ref.shape
    rows_near = near_ref.shape[0]
    tile = 512

    att_p_ref[...] = mm(att_ref[...], perm_att_ref[...]).astype(bf16)
    first_ref[...] = x_ref[...].astype(f32) + mm(att_p_ref[...], w_out_ref[...])

    normed, _ = centre_scale(first_ref[...])
    hidden = (normed * norms_ref[2:3, :] + norms_ref[3:4, :]).astype(bf16)
    hid_p_ref[...] = mm(hidden, perm_ref[...]).astype(bf16)
    cross_q_ref[...] = mm(hid_p_ref[...], w_cq_ref[...]).astype(bf16)

    @pl.loop(0, rows_near // tile)
    def _(step):
        rows = rows_of(step, tile)
        near_p_ref[rows, :] = mm(near_ref[rows, :], perm_ref[...]).astype(bf16)
        near_kv_ref[rows, :dim] = mm(near_p_ref[rows, :], w_ck_ref[...]).astype(bf16)
        near_kv_ref[rows, dim:] = mm(near_p_ref[rows, :], w_cv_ref[...]).astype(bf16)

    @pl.loop(0, spans)
    def _(span):
        span_forward(span, spans, neighbours, presence_ref, cross_q_ref, near_kv_ref, cross_ref)

    co_p_ref[...] = mm(cross_ref[...], perm_ref[...]).astype(bf16)
    second_ref[...] = first_ref[...] + mm(co_p_ref[...], w_co_ref[...])


def column_block(rows, width, index):
    return pl.BlockSpec((rows, width), lambda *_: (0, index), pipeline_mode=pl.Buffered(1))


def whole(array):
    return pl.BlockSpec(array.shape, lambda *_: (0,) * array.ndim, pipeline_mode=pl.Buffered(1))


def whole_shape(shape):
    return pl.BlockSpec(shape, lambda *_: (0,) * len(shape), pipeline_mode=pl.Buffered(1))


def cross_forward(spans, neighbours, presence, att, x, norms, perm, perm_att, near, weights):
    count, dim = x.shape
    rows_near = near.shape[0]
    out_shape = (
        jax.ShapeDtypeStruct((count, dim), bf16),
        jax.ShapeDtypeStruct((count, dim), f32),
        jax.ShapeDtypeStruct((count, dim), bf16),
        jax.ShapeDtypeStruct((count, dim), bf16),
        jax.ShapeDtypeStruct((rows_near, dim), bf16),
        jax.ShapeDtypeStruct((rows_near, 2 * dim), bf16),
        jax.ShapeDtypeStruct((count, dim), bf16),
        jax.ShapeDtypeStruct((count, dim), f32),
    )
    operands = (att, x, norms, perm, perm_att, near)
    return pl.pallas_call(
        partial(cross_forward_kernel, spans, neighbours),
        out_shape=out_shape,
        grid=(1,),
        in_specs=[pl.BlockSpec(memory_space=pltpu.SMEM)]
        + [whole(op) for op in operands]
        + [column_block(dim, dim, index) for index in (3, 4, 5, 6, 7)],
        out_specs=tuple(whole_shape(shape.shape) for shape in out_shape),
        scratch_shapes=[pltpu.VMEM((count, dim), bf16)],
        compiler_params=params(),
        name="cross_forward",
    )(presence, *operands, *([weights] * 5))


def feed_kernel(
    second_ref,
    cot_ref,
    norms_ref,
    perm_ref,
    w_up_ref,
    w_down_ref,
    out_ref,
    gsecond_ref,
    all_ref,
    gnorm_ref,
    hid_p_ref,
    hid_t_ref,
    cot_p_ref,
    cot_t_ref,
    result_ref,
    back_ref,
    gup_ref,
    gdown_ref,
    sems,
):
    step = pl.program_id(0)
    last = pl.num_programs(0) - 1
    slot = lax.rem(step, 2)
    dim, tile = w_up_ref.shape

    def copies(step, slot):
        up = pl.multiple_of(8 * dim + step * tile, tile)
        down = pl.multiple_of(8 * dim + (last + 1 + step) * tile, tile)
        return (
            pltpu.make_async_copy(gup_ref.at[slot], all_ref.at[:, pl.ds(up, tile)], sems.at[0, slot]),
            pltpu.make_async_copy(
                gdown_ref.at[slot], all_ref.at[:, pl.ds(down, tile)], sems.at[1, slot]
            ),
        )

    @pl.when(step >= 2)
    def _():
        for copy in copies(step - 2, slot):
            copy.wait()

    @pl.when(step == 0)
    def _():
        normed, _ = centre_scale(second_ref[...])
        hidden = (normed * norms_ref[4:5, :] + norms_ref[5:6, :]).astype(bf16)
        hid_p_ref[...] = mm(hidden, perm_ref[...]).astype(bf16)
        hid_t_ref[...] = hid_p_ref[...].T
        cot_p_ref[...] = mm(cot_ref[...], perm_ref[...]).astype(bf16)
        cot_t_ref[...] = cot_p_ref[...].T
        result_ref[...] = jnp.zeros_like(result_ref)
        back_ref[...] = jnp.zeros_like(back_ref)

    upward = mm(hid_p_ref[...], w_up_ref[...])
    active, slope = gelu_parts(upward)
    active = active.astype(bf16)
    result_ref[...] += nt(active, w_down_ref[...])
    gdown_ref[slot] = mm(cot_t_ref[...], active).astype(bf16)
    grad_up = (mm(cot_p_ref[...], w_down_ref[...]) * slope).astype(bf16)
    gup_ref[slot] = mm(hid_t_ref[...], grad_up).astype(bf16)
    for copy in copies(step, slot):
        copy.start()
    back_ref[...] += nt(grad_up, w_up_ref[...])

    @pl.when(step == last)
    def _():
        out_ref[...] = (
            second_ref[...] + nt(result_ref[...].astype(bf16), perm_ref[...])
        ).astype(bf16)
        upstream = nt(back_ref[...].astype(bf16), perm_ref[...])
        normed, recip = centre_scale(second_ref[...])
        back, gain, shift = norm_back(upstream, normed, recip, norms_ref[4:5, :])
        gsecond_ref[...] = cot_ref[...].astype(f32) + back
        gnorm_ref[0:1, :] = gain
        gnorm_ref[1:2, :] = shift
        for which in (step - 1, step):
            for copy in copies(which, lax.rem(which, 2)):
                copy.wait()


def feed(second, cot, norms, perm, weights):
    count, dim = second.shape
    ffw = (weights.shape[1] - 8 * dim) // 2
    tile = 512
    first_up = 8 * dim // tile
    first_down = (8 * dim + ffw) // tile
    out_shape = (
        jax.ShapeDtypeStruct((count, dim), bf16),
        jax.ShapeDtypeStruct((count, dim), f32),
        jax.ShapeDtypeStruct(weights.shape, bf16),
        jax.ShapeDtypeStruct((2, dim), f32),
    )
    operands = (second, cot, norms, perm)
    return pl.pallas_call(
        feed_kernel,
        out_shape=out_shape,
        grid=(ffw // tile,),
        in_specs=[whole(op) for op in operands]
        + [
            pl.BlockSpec((dim, tile), lambda i: (0, first_up + i)),
            pl.BlockSpec((dim, tile), lambda i: (0, first_down + i)),
        ],
        out_specs=(
            whole_shape((count, dim)),
            whole_shape((count, dim)),
            pl.BlockSpec(memory_space=pl.ANY),
            whole_shape((2, dim)),
        ),
        scratch_shapes=[
            pltpu.VMEM((count, dim), bf16),
            pltpu.VMEM((dim, count), bf16),
            pltpu.VMEM((count, dim), bf16),
            pltpu.VMEM((dim, count), bf16),
            pltpu.VMEM((count, dim), f32),
            pltpu.VMEM((count, dim), f32),
            pltpu.VMEM((2, dim, tile), bf16),
            pltpu.VMEM((2, dim, tile), bf16),
            pltpu.SemaphoreType.DMA((2, 2)),
        ],
        compiler_params=params(),
        name="feed",
    )(*operands, weights, weights)


def cross_backward_kernel(
    spans,
    neighbours,
    lines,
    presence_ref,
    gsecond_ref,
    first_ref,
    norms_ref,
    perm_ref,
    perm_att_ref,
    att_p_ref,
    hid_p_ref,
    cross_q_ref,
    near_p_ref,
    near_kv_ref,
    co_p_ref,
    w_out_ref,
    w_cq_ref,
    w_co_ref,
    _,
    gfirst_ref,
    gatt_ref,
    all_ref,
    gnorm_ref,
    *rest,
):
    count, dim = first_ref.shape
    rows_near = near_p_ref.shape[0]
    span_len = count // spans
    near = rows_near // spans
    group = 256 // HEAD
    outs = []
    if lines:
        gatt_tok_ref, row_sems, send_sems = rest[5:]
        place = Place(lines)
        place.meet()
        send = Sender(place, send_sems)
    gco_ref, gcq_ref, gnear_ref, gw_ref, sems = rest[:5]

    def keep(index, value):
        slot = len(outs) % 3
        if len(outs) >= 3:
            outs[-3].wait()
        gw_ref[slot] = value.astype(bf16)
        outs.append(
            pltpu.make_async_copy(
                gw_ref.at[slot],
                all_ref.at[:, pl.ds((3 + index) * dim, dim)],
                sems.at[index],
            )
        )
        outs[-1].start()

    upper = gsecond_ref[...].astype(bf16)
    gco_ref[...] = nt(nt(upper, w_co_ref[...]).astype(bf16), perm_ref[...]).astype(bf16)

    def one_span(span):
        rows = rows_of(span, span_len)
        keys = rows_of(span, near)
        live, anyone = live_keys(presence_ref, span, (near, 1), 0, neighbours, near // neighbours)
        for begin in range(0, dim, group * HEAD):
            lanes = slice(begin, begin + group * HEAD)
            lanes_v = slice(dim + begin, dim + begin + group * HEAD)
            query = spread_heads(cross_q_ref[rows, lanes] * SCALE, span_len, group)
            grad_out = spread_heads(gco_ref[rows, lanes], span_len, group)
            key = near_kv_ref[keys, lanes]
            scores = jnp.where(live > 0, nt(key, query), masked_score)
            peak = jnp.max(scores, axis=0, keepdims=True)
            expon = jnp.exp(scores - peak) * live
            total = jnp.sum(expon, axis=0, keepdims=True) + 1.0 - anyone
            probs = expon * (1.0 / total)
            grad_probs = nt(near_kv_ref[keys, lanes_v], grad_out)
            inner = jnp.sum(probs * grad_probs, axis=0, keepdims=True)
            grad_scores = (probs * (grad_probs - inner)).astype(bf16)
            gcq_ref[rows, lanes] = (
                gather_heads(tn(grad_scores, key), span_len, group) * SCALE
            ).astype(bf16)
            gnear_ref[keys, lanes] = mm(grad_scores, query).astype(bf16)
            gnear_ref[keys, lanes_v] = mm(probs.astype(bf16), grad_out).astype(bf16)

    pl.loop(0, spans)(one_span)

    upstream = nt(nt(gcq_ref[...], w_cq_ref[...]).astype(bf16), perm_ref[...])
    normed, recip = centre_scale(first_ref[...])
    back, gain, shift = norm_back(upstream, normed, recip, norms_ref[2:3, :])
    gnorm_ref[0:1, :] = gain
    gnorm_ref[1:2, :] = shift
    gfirst_ref[...] = gsecond_ref[...] + back
    lower = gfirst_ref[...].astype(bf16)
    gatt = nt(nt(lower, w_out_ref[...]).astype(bf16), perm_att_ref[...]).astype(bf16)
    if lines:
        width = gatt_ref.shape[1]
        tokens = gatt_ref.shape[0] // 8
        shares = gatt.shape[1] // width
        gatt_tok_ref[...] = gatt

        def block(device):
            return gatt_tok_ref.at[
                pl.ds(pl.multiple_of(device // shares * tokens, tokens), tokens),
                pl.ds(pl.multiple_of(device % shares * width, width), width),
            ]

        def landing(device):
            return gatt_ref.at[pl.ds(pl.multiple_of(device * tokens, tokens), tokens)]

        for other in place.plane():
            send.start(None, block(other), landing(place.me), row_sems.at[place.me], seq=other)
        own = pltpu.make_async_copy(block(place.me), landing(place.me), row_sems.at[place.me])
        own.start()
    else:
        gatt_ref[...] = gatt
    keep(4, mm(co_p_ref[...].T, upper))
    near_t = near_p_ref[...].T
    for part in range(2):
        keep(2 + part, mm(near_t, gnear_ref[:, part * dim : (part + 1) * dim]))
    keep(1, mm(hid_p_ref[...].T, gcq_ref[...]))
    keep(0, mm(att_p_ref[...].T, lower))
    if lines:
        for other in place.plane():
            send.arrived(None, landing(other), row_sems.at[other])
        own.wait()
        send.finish()
    for copy in outs[-3:]:
        copy.wait()


def cross_backward(
    spans,
    neighbours,
    lines,
    presence,
    gsecond,
    first,
    norms,
    perm,
    perm_att,
    att_p,
    hid_p,
    cross_q,
    near_p,
    near_kv,
    co_p,
    weights,
    grads,
):
    count, dim = first.shape
    rows_near = near_p.shape[0]
    gatt_shape = (count, perm_att.shape[0])
    out_shape = [
        jax.ShapeDtypeStruct((count, dim), f32),
        jax.ShapeDtypeStruct(gatt_shape, bf16),
        jax.ShapeDtypeStruct(grads.shape, bf16),
        jax.ShapeDtypeStruct((2, dim), f32),
    ]
    scratch = [
        pltpu.VMEM((count, dim), bf16),
        pltpu.VMEM((count, dim), bf16),
        pltpu.VMEM((rows_near, 2 * dim), bf16),
        pltpu.VMEM((3, dim, dim), bf16),
        pltpu.SemaphoreType.DMA((5,)),
    ]
    compiler_params = params()
    if lines:
        out_shape[1] = jax.ShapeDtypeStruct((2 * count, gatt_shape[1] // 2), bf16)
        scratch += [
            pltpu.VMEM(gatt_shape, bf16),
            pltpu.SemaphoreType.DMA((8,)),
            pltpu.SemaphoreType.DMA((8,)),
        ]
        compiler_params = pltpu.CompilerParams(
            vmem_limit_bytes=VMEM_BYTES, collective_id=2, has_side_effects=True
        )
    operands = (
        gsecond,
        first,
        norms,
        perm,
        perm_att,
        att_p,
        hid_p,
        cross_q,
        near_p,
        near_kv,
        co_p,
    )
    return pl.pallas_call(
        partial(cross_backward_kernel, spans, neighbours, lines),
        out_shape=out_shape,
        grid=(1,),
        in_specs=[pl.BlockSpec(memory_space=pltpu.SMEM)]
        + [whole(op) for op in operands]
        + [column_block(dim, dim, index) for index in (3, 4, 7)]
        + [pl.BlockSpec(memory_space=pl.ANY)],
        out_specs=tuple(
            pl.BlockSpec(memory_space=pl.ANY) if index == 2 else whole_shape(shape.shape)
            for index, shape in enumerate(out_shape)
        ),
        scratch_shapes=scratch,
        input_output_aliases={len(operands) + 4: 2},
        compiler_params=compiler_params,
        name="cross_backward",
    )(presence, *operands, *([weights] * 3), grads)


def last_norm_kernel(parts_ref, x_ref, gfirst_ref, norms_ref, perm_ref, out_ref, gnorm_ref):
    total = parts_ref[0].astype(f32)
    for part in range(1, parts_ref.shape[0]):
        total = total + parts_ref[part].astype(f32)
    upstream = nt(total.astype(bf16), perm_ref[...])
    normed, recip = centre_scale(x_ref[...].astype(f32))
    back, gain, shift = norm_back(upstream, normed, recip, norms_ref[0:1, :])
    out_ref[...] = gfirst_ref[...] + back
    gnorm_ref[0:1, :] = gain
    gnorm_ref[1:2, :] = shift


def last_norm(parts, x, gfirst, norms, perm):
    count, dim = x.shape
    return pl.pallas_call(
        last_norm_kernel,
        out_shape=(
            jax.ShapeDtypeStruct((count, dim), f32),
            jax.ShapeDtypeStruct((2, dim), f32),
        ),
        compiler_params=params(),
        name="last_norm",
    )(parts, x, gfirst, norms, perm)


def forward_kernel(
    lines,
    pairs,
    spans,
    neighbours,
    presence_ref,
    w_ref,
    norm_ref,
    x_ref,
    perm_ref,
    cot_ref,
    near_ref,
    wts_ref,
    all_ref,
    hid_out,
    qkv_out,
    att_out,
    lse_out,
    att_p_out,
    first_out,
    hid_p_out,
    cross_q_out,
    near_p_out,
    near_kv_out,
    co_p_out,
    norms_ref,
    out_ref,
    gsecond_ref,
    gnorm_ref,
    *scratch,
):
    results, scratch = scratch[:11], scratch[11:]
    (
        hid_ref,
        qkv_ref,
        att_ref,
        lse_ref,
        att_p_ref,
        first_ref,
        hid_p_ref,
        cross_q_ref,
        near_p_ref,
        near_kv_ref,
        co_p_ref,
    ) = results
    work, scratch = scratch[:15], scratch[15:]
    (
        second_ref,
        own_ref,
        small_ref,
        rows_ref,
        w_qkv_ref,
        w_mid_ref,
        att_tok_ref,
        cross_ref,
        up_p_ref,
        up_t_ref,
        cot_p_ref,
        cot_t_ref,
        result_ref,
        back_ref,
        gfeed_ref,
    ) = work
    (
        send_sems,
        z_sems,
        y_sems,
        x_sems,
        a_sems,
        b_sems,
        sib_sems,
        norm_sems,
        row_sems,
        att_sems,
        local_sems,
        qkv_sems,
        mid_sems,
        feed_sems,
        out_sems,
    ) = scratch
    place = Place(lines)
    z, me, core = place.z, place.me, place.core
    length, dim = hid_ref.shape
    width = pairs * LANES
    tokens = length // 8
    half = own_ref.shape[0] // 2
    near_load = pltpu.make_async_copy(near_ref, near_p_ref, local_sems.at[2])
    near_load.start()
    own_ref[...] = w_ref[...].astype(bf16)
    place.meet()
    send = Sender(place, send_sems)
    unit = partial(unit_of, wts_ref, lines)
    events = place.events()
    keep = pltpu.make_async_copy(own_ref, unit(z, me), local_sems.at[0])
    keep.start()

    def obtain(index):
        condition, line, far, side = events[index]
        mine = unit(line, me)
        src = own_ref if far == 0 else mine
        if far:
            send.arrived(condition, mine, z_sems.at[line])
        if side >= 0:
            send.start(both(condition, z > 0), src, mine, z_sems.at[line], z=z - 1)
        if side <= 0:
            send.start(both(condition, z < lines - 1), src, mine, z_sems.at[line], z=z + 1)
        send.start(condition, src, mine, x_sems.at[line], seq=place.xn)
        send.start(condition, src, mine, y_sems.at[line], seq=place.yn)
        send.start(condition, src, mine, sib_sems.at[0, line], seq=place.sib)

    def pass_on(index):
        condition, line, _, _ = events[index]
        from_x, from_y = unit(line, place.xn), unit(line, place.yn)
        send.arrived(condition, from_x, x_sems.at[line])
        part = unit(line, place.xn, half, half)
        send.start(condition, part, part, b_sems.at[line], seq=place.yn)
        send.start(condition, from_x, from_x, sib_sems.at[1, line], seq=place.sib)
        send.arrived(condition, from_y, y_sems.at[line])
        part = unit(line, place.yn, 0, half)
        send.start(condition, part, part, a_sems.at[line], seq=place.xn)
        send.start(condition, from_y, from_y, sib_sems.at[2, line], seq=place.sib)

    def corner(index):
        condition, line, _, _ = events[index]
        for group, begin, sems in ((3, 0, a_sems), (4, half, b_sems)):
            part = unit(line, place.dg, begin, half)
            send.arrived(condition, part, sems.at[line])
            send.start(condition, part, part, sib_sems.at[group, line], seq=place.sib)

    kept = []

    def emit(index):
        out = (
            hid_out,
            qkv_out,
            att_out,
            lse_out,
            att_p_out,
            first_out,
            hid_p_out,
            cross_q_out,
            near_p_out,
            near_kv_out,
            co_p_out,
        )[index]
        kept.append(pltpu.make_async_copy(results[index], out, out_sems.at[index]))
        kept[-1].start()

    def row_block(seq):
        return rows_ref.at[pl.ds(pl.multiple_of(seq * tokens, tokens), tokens)]

    def middle(index):
        return pltpu.make_async_copy(
            wts_ref.at[:, pl.ds((3 + index) * dim, dim)], w_mid_ref.at[index], mid_sems.at[index]
        )

    obtain(0)
    own_rows = pltpu.make_async_copy(x_ref.at[place.chip], row_block(me), local_sems.at[1])
    own_rows.start()
    others = (place.xn, place.yn, place.dg)
    for other in place.line():
        send.start(None, norm_ref, small_ref.at[z], norm_sems.at[z], z=other)
    small_ref[z] = norm_ref[...]
    send.start(None, x_ref.at[place.chip], row_block(me), row_sems.at[me], seq=place.sib)
    for other in others:
        send.start(None, x_ref.at[other // 2], row_block(me), row_sems.at[me], seq=other)
    near_load.wait()

    @pl.loop(0, near_p_ref.shape[0] // 512)
    def _(step):
        rows = rows_of(step, 512)
        near_p_ref[rows, :] = mm(near_p_ref[rows, :], perm_ref[...]).astype(bf16)

    emit(8)
    obtain(1)
    obtain(2)
    pass_on(0)
    for other in others:
        send.arrived(None, row_block(other), row_sems.at[other])
        send.start(None, row_block(other), row_block(other), row_sems.at[other], seq=place.sib)
    obtain(3)
    obtain(4)
    cot_p_ref[...] = mm(cot_ref[...], perm_ref[...]).astype(bf16)
    cot_t_ref[...] = cot_p_ref[...].T
    pass_on(1)
    pass_on(2)
    corner(0)

    for other in place.line():
        send.arrived(None, small_ref.at[other], norm_sems.at[other])
    piece = small_ref.shape[2]
    total = None
    for line in range(lines):
        row = lax.broadcasted_iota(jnp.int32, (piece, dim), 0)
        column = lax.broadcasted_iota(jnp.int32, (piece, dim), 1)
        part = dim // lines
        place_of = jnp.logical_and(row < part, column == row + line * part).astype(bf16)
        term = mm(small_ref[line], place_of)
        total = term if total is None else total + term
    norms_ref[...] = total[: norms_ref.shape[0]]

    last = len(events)
    for index in range(5, last, 2):
        obtain(index)
        obtain(index + 1)
        if index == 5:
            for other in others:
                theirs = other + 1 - 2 * core
                send.arrived(None, row_block(theirs), row_sems.at[theirs])
            send.arrived(None, row_block(place.sib), row_sems.at[place.sib])
            own_rows.wait()
            norm_rows(rows_ref, norms_ref[...], perm_ref, hid_ref)
            emit(0)
        pass_on(index - 2)
        pass_on(index - 1)
        corner(index - 4)
        corner(index - 3)
    for index in range(last - 2, last):
        pass_on(index)
    for index in range(last - 4, last):
        corner(index)
    keep.wait()
    for line in range(lines):
        for group, first in enumerate((me, place.xn, place.yn)):
            theirs = first + 1 - 2 * core
            send.arrived(None, unit(line, theirs), sib_sems.at[group, line])
        theirs = place.dg + 1 - 2 * core
        send.arrived(None, unit(line, theirs, 0, half), sib_sems.at[3, line])
        send.arrived(None, unit(line, theirs, half, half), sib_sems.at[4, line])
    copies = weight_copies(pairs, dim, wts_ref, w_qkv_ref, qkv_sems)
    for copy in copies + [middle(index) for index in (2, 3, 0, 1, 4)]:
        copy.start()
    for part in range(3):
        copies[part].wait()
        triple_part(part, pairs, hid_ref, w_qkv_ref, qkv_ref)
    emit(1)

    share = lax.rem(me, dim // width)
    seq_rows = pl.ds(pl.multiple_of(place.chip * tokens, tokens), tokens)

    def landing(pair, chip_rows, share):
        lanes = pl.ds(pl.multiple_of(share * width + pair * LANES, LANES), LANES)
        return att_tok_ref.at[chip_rows, lanes]

    for pair in range(pairs):
        lanes = slice(pair * LANES, (pair + 1) * LANES)
        pair_forward(pair, pairs, qkv_ref, att_ref, lse_ref, lambda: None)
        for other in place.plane():
            block = att_ref.at[pl.ds(pl.multiple_of(other * tokens, tokens), tokens), lanes]
            to = landing(pair, seq_rows, share)
            send.start(None, block, to, att_sems.at[pair, me], seq=other)
        own_block = att_ref[pl.ds(pl.multiple_of(me * tokens, tokens), tokens), lanes]
        landing(pair, seq_rows, share)[...] = own_block
    emit(2)
    emit(3)

    for index in (2, 3, 0, 1, 4):
        middle(index).wait()
    for step in range(near_p_ref.shape[0] // 512):
        rows = slice(step * 512, (step + 1) * 512)
        near_kv_ref[rows, :dim] = mm(near_p_ref[rows, :], w_mid_ref[2]).astype(bf16)
        near_kv_ref[rows, dim:] = mm(near_p_ref[rows, :], w_mid_ref[3]).astype(bf16)
    emit(9)
    w_out_ref, w_cq_ref, w_co_ref = (w_mid_ref.at[index] for index in (0, 1, 4))
    for pair in range(pairs):
        for other in place.plane():
            rows = pl.ds(pl.multiple_of(other // 2 * tokens, tokens), tokens)
            send.arrived(None, landing(pair, rows, lax.rem(other, 2)), att_sems.at[pair, other])
    att_p_ref[...] = mm(att_tok_ref[...], perm_ref[...]).astype(bf16)
    emit(4)
    own_x = x_ref[...].reshape(first_ref.shape).astype(f32)
    first_ref[...] = own_x + mm(att_p_ref[...], w_out_ref[...])
    emit(5)
    normed, _ = centre_scale(first_ref[...])
    hidden = (normed * norms_ref[2:3, :] + norms_ref[3:4, :]).astype(bf16)
    hid_p_ref[...] = mm(hidden, perm_ref[...]).astype(bf16)
    emit(6)
    cross_q_ref[...] = mm(hid_p_ref[...], w_cq_ref[...]).astype(bf16)
    emit(7)
    pl.loop(0, spans)(
        lambda span: span_forward(
            span, spans, neighbours, presence_ref, cross_q_ref, near_kv_ref, cross_ref
        )
    )

    ffw = (all_ref.shape[1] - 8 * dim) // 2
    tile = gfeed_ref.shape[2]
    order = range(0, ffw, tile)

    def tile_load(index):
        return [
            pltpu.make_async_copy(
                wts_ref.at[:, pl.ds(8 * dim + part * ffw + order[index], tile)],
                w_mid_ref.at[(2 * index + part) % 4],
                feed_sems.at[0, (2 * index + part) % 4],
            )
            for part in range(2)
        ]

    def tile_store(index):
        return [
            pltpu.make_async_copy(
                gfeed_ref.at[(2 * index + part) % 4],
                all_ref.at[:, pl.ds(8 * dim + part * ffw + order[index], tile)],
                feed_sems.at[1, (2 * index + part) % 4],
            )
            for part in range(2)
        ]

    for copy in tile_load(0) + tile_load(1):
        copy.start()
    co_p_ref[...] = mm(cross_ref[...], perm_ref[...]).astype(bf16)
    emit(10)
    second_ref[...] = first_ref[...] + mm(co_p_ref[...], w_co_ref[...])
    normed, _ = centre_scale(second_ref[...])
    hidden = (normed * norms_ref[4:5, :] + norms_ref[5:6, :]).astype(bf16)
    up_p_ref[...] = mm(hidden, perm_ref[...]).astype(bf16)
    up_t_ref[...] = up_p_ref[...].T

    for index in range(len(order)):
        up_ref, down_ref = w_mid_ref.at[2 * index % 4], w_mid_ref.at[2 * index % 4 + 1]
        for copy in tile_load(index):
            copy.wait()
        if index >= 2:
            for copy in tile_store(index - 2):
                copy.wait()
        active, slope = gelu_parts(mm(up_p_ref[...], up_ref[...]))
        active = active.astype(bf16)
        term = nt(active, down_ref[...])
        result_ref[...] = term if index == 0 else result_ref[...] + term
        gfeed_ref[2 * index % 4 + 1] = mm(cot_t_ref[...], active).astype(bf16)
        grad_up = (mm(cot_p_ref[...], down_ref[...]) * slope).astype(bf16)
        gfeed_ref[2 * index % 4] = mm(up_t_ref[...], grad_up).astype(bf16)
        for copy in tile_store(index):
            copy.start()
        term = nt(grad_up, up_ref[...])
        back_ref[...] = term if index == 0 else back_ref[...] + term
        if index + 2 < len(order):
            for copy in tile_load(index + 2):
                copy.start()

    out_ref[...] = (second_ref[...] + nt(result_ref[...].astype(bf16), perm_ref[...])).astype(bf16)
    upstream = nt(back_ref[...].astype(bf16), perm_ref[...])
    normed, recip = centre_scale(second_ref[...])
    back, gain, shift = norm_back(upstream, normed, recip, norms_ref[4:5, :])
    gsecond_ref[...] = cot_ref[...].astype(f32) + back
    gnorm_ref[0:1, :] = gain
    gnorm_ref[1:2, :] = shift
    for index in range(len(order) - 2, len(order)):
        for copy in tile_store(index):
            copy.wait()
    for copy in kept:
        copy.wait()
    send.finish()


def forward(lines, pairs, spans, neighbours, presence, w_shard, n_shard, inputs, perm, cot, near):
    unit_rows, unit_cols = w_shard.shape
    seqs, tokens, dim = inputs.shape
    count, length, width = seqs * tokens, 8 * tokens, pairs * LANES
    rows_near = near.shape[0]
    events = 2 * lines - 1
    any_space = pl.BlockSpec(memory_space=pl.ANY)
    vmem = pl.BlockSpec(memory_space=pltpu.VMEM)
    dma = pltpu.SemaphoreType.DMA
    packed = jax.ShapeDtypeStruct((unit_rows * lines, unit_cols * 8), bf16)
    kept = (
        ((length, dim), bf16),
        ((3 * pairs, length, LANES), bf16),
        ((length, width), bf16),
        ((pairs, 2, length), f32),
        ((count, dim), bf16),
        ((count, dim), f32),
        ((count, dim), bf16),
        ((count, dim), bf16),
        ((rows_near, dim), bf16),
        ((rows_near, 2 * dim), bf16),
        ((count, dim), bf16),
    )
    tile = unit_cols // 2
    return pl.pallas_call(
        partial(forward_kernel, lines, pairs, spans, neighbours),
        out_shape=(packed, packed)
        + tuple(jax.ShapeDtypeStruct(*entry) for entry in kept)
        + (
            jax.ShapeDtypeStruct((8, dim), f32),
            jax.ShapeDtypeStruct((count, dim), bf16),
            jax.ShapeDtypeStruct((count, dim), f32),
            jax.ShapeDtypeStruct((2, dim), f32),
        ),
        in_specs=[pl.BlockSpec(memory_space=pltpu.SMEM)] + [vmem] * 5 + [any_space],
        out_specs=(any_space,) * (2 + len(kept)) + (vmem,) * 4,
        scratch_shapes=[pltpu.VMEM(*entry) for entry in kept]
        + [
            pltpu.VMEM((count, dim), f32),
            pltpu.VMEM((unit_rows, unit_cols), bf16),
            pltpu.VMEM((lines,) + n_shard.shape, bf16),
            pltpu.VMEM((length, dim), bf16),
            pltpu.VMEM((dim, 3 * width), bf16),
            pltpu.VMEM((5, dim, dim), bf16),
            pltpu.VMEM((count, dim), bf16),
            pltpu.VMEM((count, dim), bf16),
            pltpu.VMEM((count, dim), bf16),
            pltpu.VMEM((dim, count), bf16),
            pltpu.VMEM((count, dim), bf16),
            pltpu.VMEM((dim, count), bf16),
            pltpu.VMEM((count, dim), f32),
            pltpu.VMEM((count, dim), f32),
            pltpu.VMEM((4, dim, tile), bf16),
            dma((11 * events + 7 + lines + 7 * pairs,)),
            dma((lines,)),
            dma((lines,)),
            dma((lines,)),
            dma((lines,)),
            dma((lines,)),
            dma((5, lines)),
            dma((lines,)),
            dma((8,)),
            dma((pairs, 8)),
            dma((3,)),
            dma((3,)),
            dma((5,)),
            dma((2, 4)),
            dma((len(kept),)),
        ],
        compiler_params=pltpu.CompilerParams(
            vmem_limit_bytes=VMEM_BYTES, collective_id=1, has_side_effects=True
        ),
        name="forward",
    )(presence, w_shard, n_shard, inputs, perm, cot, near)


def reduce_kernel(
    lines,
    grads_ref,
    small_ref,
    shard_ref,
    norms_ref,
    mine_ref,
    sib_ref,
    corner_a_ref,
    corner_b_ref,
    from_x_ref,
    from_y_ref,
    below_ref,
    above_ref,
    plane_ref,
    plane_sum_ref,
    line_ref,
    send_sems,
    load_sems,
    sib_sems,
    a_sems,
    b_sems,
    x_sems,
    y_sems,
    below_sems,
    above_sems,
    plane_sems,
    line_sems,
):
    place = Place(lines)
    z, me = place.z, place.me
    unit_rows, unit_cols = shard_ref.shape
    half = unit_rows // 2
    tile = 32
    place.meet()
    send = Sender(place, send_sems)
    chips = (place.dg, place.yn, place.xn, me)
    corner, over_y, over_x, here = range(4)

    unit = partial(unit_of, grads_ref, lines)

    def load(which, line):
        return pltpu.make_async_copy(
            unit(line, chips[which]), mine_ref.at[which, line], load_sems.at[which, line]
        )

    for other in place.plane():
        send.start(None, small_ref, plane_ref.at[me], plane_sems.at[me], seq=other)
    plane_ref[me] = small_ref[...]

    events = place.events()[::-1]
    for condition, line, _, _ in events:
        for which in range(4):
            theirs = chips[which] + 1 - 2 * place.core
            send.start(
                condition,
                unit(line, theirs),
                sib_ref.at[which, line],
                sib_sems.at[which, line],
                seq=place.sib,
            )
            when(condition, load(which, line).start)

    def add(target, *terms, begin=0, size=unit_rows):
        @pl.loop(0, size // tile)
        def _(step):
            rows = pl.ds(pl.multiple_of(begin + step * tile, tile), tile)
            if len(terms) == 1:
                ref, first = terms[0]
                at = pl.ds(pl.multiple_of(begin - first + step * tile, tile), tile)
                target[rows, :] = target[rows, :] + ref[at, :]
            else:
                total = target[rows, :].astype(f32)
                for ref, first in terms:
                    at = pl.ds(pl.multiple_of(begin - first + step * tile, tile), tile)
                    total = total + ref[at, :].astype(f32)
                target[rows, :] = total.astype(target.dtype)

    def own(which, index):
        condition, line, _, _ = events[index]
        send.arrived(condition, sib_ref.at[which, line], sib_sems.at[which, line])
        when(condition, load(which, line).wait)

    def first(index):
        condition, line, _, _ = events[index]
        own(corner, index)
        target = mine_ref.at[corner, line]
        when(condition, lambda: add(target, (sib_ref.at[corner, line], 0)))
        send.start(
            condition,
            target.at[pl.ds(0, half)],
            corner_a_ref.at[line],
            a_sems.at[line],
            seq=place.xn,
        )
        send.start(
            condition,
            target.at[pl.ds(half, half)],
            corner_b_ref.at[line],
            b_sems.at[line],
            seq=place.yn,
        )

    def second(index):
        condition, line, _, _ = events[index]
        for which, part, sems, begin, to, landing, landing_sems in (
            (over_y, corner_a_ref, a_sems, 0, place.yn, from_y_ref, y_sems),
            (over_x, corner_b_ref, b_sems, half, place.xn, from_x_ref, x_sems),
        ):
            own(which, index)
            send.arrived(condition, part.at[line], sems.at[line])
            target = mine_ref.at[which, line]

            def body(which=which, part=part, begin=begin, target=target):
                add(
                    target,
                    (sib_ref.at[which, line], 0),
                    (part.at[line], begin),
                    begin=begin,
                    size=half,
                )
                add(target, (sib_ref.at[which, line], 0), begin=half - begin, size=half)

            when(condition, body)
            send.start(condition, target, landing.at[line], landing_sems.at[line], seq=to)

    def third(index):
        condition, line, far, side = events[index]
        own(here, index)
        send.arrived(condition, from_x_ref.at[line], x_sems.at[line])
        send.arrived(condition, from_y_ref.at[line], y_sems.at[line])
        target = mine_ref.at[here, line]
        terms = [(ref.at[line], 0) for ref in (sib_ref.at[here], from_x_ref, from_y_ref)]
        if side == 0:
            has_below, has_above = z > 0, z < lines - 1
            add(target, *terms)
            send.arrived(has_below, below_ref.at[line], below_sems.at[line])
            send.arrived(has_above, above_ref.at[line], above_sems.at[line])

            @pl.loop(0, unit_rows // tile)
            def _(step):
                rows = rows_of(step, tile)
                shard_ref[rows, :] = target[rows, :].astype(f32)

            when(has_below, lambda: add(shard_ref, (below_ref.at[line], 0)))
            when(has_above, lambda: add(shard_ref, (above_ref.at[line], 0)))
            return
        landing, sems = (below_ref, below_sems) if side > 0 else (above_ref, above_sems)
        more = both(condition, z > 0) if side > 0 else both(condition, z < lines - 1)
        none = both(condition, z == 0) if side > 0 else both(condition, z == lines - 1)
        send.arrived(more, landing.at[line], sems.at[line])
        when(more, lambda: add(target, *terms, (landing.at[line], 0)))
        when(none, lambda: add(target, *terms))
        send.start(condition, target, landing.at[line], sems.at[line], z=z + side)

    count = len(events)
    first(0)
    first(1)
    for index in range(2, count + 4):
        if index < count:
            first(index)
        if 0 <= index - 2 < count:
            second(index - 2)
        if index == 3:
            for other in place.plane():
                send.arrived(None, plane_ref.at[other], plane_sems.at[other])
            total = plane_ref[0]
            for other in range(1, 8):
                total = total + plane_ref[other]
            plane_sum_ref[...] = total
            line_ref[z] = total
            for other in place.line():
                send.start(None, plane_sum_ref, line_ref.at[z], line_sems.at[z], z=other)
        if 0 <= index - 4 < count:
            third(index - 4)

    for other in place.line():
        send.arrived(None, line_ref.at[other], line_sems.at[other])
    total = line_ref[0]
    for other in range(1, lines):
        total = total + line_ref[other]
    norms_ref[...] = total
    send.finish()


def reduce_grads(lines, grads, small):
    rows, cols = grads.shape
    unit_rows, unit_cols = rows // lines, cols // 8
    half = unit_rows // 2
    any_space = pl.BlockSpec(memory_space=pl.ANY)
    vmem = pl.BlockSpec(memory_space=pltpu.VMEM)
    dma = pltpu.SemaphoreType.DMA
    return pl.pallas_call(
        partial(reduce_kernel, lines),
        out_shape=(
            jax.ShapeDtypeStruct((unit_rows, unit_cols), f32),
            jax.ShapeDtypeStruct(small.shape, f32),
        ),
        in_specs=[any_space, vmem],
        out_specs=(vmem, vmem),
        scratch_shapes=[
            pltpu.VMEM((4, lines, unit_rows, unit_cols), bf16),
            pltpu.VMEM((4, lines, unit_rows, unit_cols), bf16),
            pltpu.VMEM((lines, half, unit_cols), bf16),
            pltpu.VMEM((lines, half, unit_cols), bf16),
            pltpu.VMEM((lines, unit_rows, unit_cols), bf16),
            pltpu.VMEM((lines, unit_rows, unit_cols), bf16),
            pltpu.VMEM((lines, unit_rows, unit_cols), bf16),
            pltpu.VMEM((lines, unit_rows, unit_cols), bf16),
            pltpu.VMEM((8,) + small.shape, f32),
            pltpu.VMEM(small.shape, f32),
            pltpu.VMEM((lines,) + small.shape, f32),
            dma((9 * (2 * lines - 1) + 7 + lines,)),
            dma((4, lines)),
            dma((4, lines)),
            dma((lines,)),
            dma((lines,)),
            dma((lines,)),
            dma((lines,)),
            dma((lines,)),
            dma((lines,)),
            dma((8,)),
            dma((lines,)),
        ],
        compiler_params=pltpu.CompilerParams(
            vmem_limit_bytes=VMEM_BYTES, collective_id=4, has_side_effects=True
        ),
        name="reduce_grads",
    )(grads, small)


def adam_update(grad, weight, first, second, average, rate, decay):
    first = beta_first * first + (1.0 - beta_first) * grad
    second = beta_second * second + (1.0 - beta_second) * grad * grad
    stepped = (
        first / (1.0 - beta_first**STEP) / (jnp.sqrt(second / (1.0 - beta_second**STEP)) + adam_eps)
    )
    weight = weight - rate * (stepped + decay * weight)
    average = ema_decay * average + (1.0 - ema_decay) * weight
    return (first, second, weight, average)


def on_device(
    inputs,
    cotangent,
    neighbours,
    presence,
    row_order,
    w_master,
    w_first,
    w_second,
    w_average,
    n_master,
    n_first,
    n_second,
    n_average,
):
    seqs, tokens, dim = inputs.shape
    heads = dim // HEAD
    devices = lax.axis_size("seq")
    count = seqs * tokens
    length = devices * tokens
    me = lax.axis_index("seq")
    shares = devices // seqs
    held = heads // shares
    pairs = (held + 1) // 2
    width = pairs * LANES
    spare = width - held * HEAD
    sequence, share = me // shares, me % shares

    lines = lax.axis_size("dp")
    planar = devices == 8 and seqs == 4 and spare == 0
    perm = (jnp.arange(dim)[:, None] == row_order[None, :]).astype(bf16)
    perm_att = perm
    if spare:
        perm_att = jnp.pad(perm.reshape(shares, held * HEAD, dim), ((0, 0), (0, spare), (0, 0)))
        perm_att = perm_att.reshape(shares * width, dim)
    x = inputs.reshape(count, dim)
    spans = seqs * neighbours.shape[1]
    each = neighbours.shape[2]
    near = neighbours.reshape(-1, dim)
    live = presence.reshape(-1)
    part = n_master.shape[1]
    if planar:
        small = jnp.pad(n_master.astype(bf16), ((0, 16 - 6), (0, -part % LANES)))
        (
            weights,
            grads,
            hid,
            qkv,
            att,
            lse,
            att_p,
            first,
            hid_p,
            cross_q,
            near_p,
            near_kv,
            co_p,
            norms,
            outputs,
            gsecond,
            gnorm_e,
        ) = forward(
            lines,
            pairs,
            spans,
            each,
            live,
            w_master,
            small,
            inputs,
            perm,
            cotangent.reshape(count, dim),
            near,
        )
    else:
        weights = lax.all_gather(w_master.astype(bf16), "dp", axis=0, tiled=True)
        weights = lax.all_gather(weights, "seq", axis=1, tiled=True)
        norms = lax.all_gather(n_master.astype(bf16), "dp", axis=1, tiled=True).astype(f32)
        rows = lax.all_to_all(jnp.repeat(inputs, shares, axis=0), "seq", 0, 0)
        rows = rows.reshape(length, dim)
        w_qkv = weights[:, : 3 * dim].reshape(dim, 3, shares, held * HEAD)
        w_qkv = lax.dynamic_index_in_dim(w_qkv, share, axis=2, keepdims=False)
        w_qkv = jnp.pad(w_qkv, ((0, 0), (0, 0), (0, spare))).reshape(dim, 3 * width)
        hid, qkv, att, lse = self_forward(pairs, rows, norms, perm, w_qkv)
        att_tok = (
            lax.all_to_all(att.reshape(devices, tokens, width), "seq", 0, 0)
            .reshape(seqs, shares, tokens, width)
            .transpose(0, 2, 1, 3)
            .reshape(count, shares * width)
        )
        att_p, first, hid_p, cross_q, near_p, near_kv, co_p, second = cross_forward(
            spans, each, live, att_tok, x, norms, perm, perm_att, near, weights
        )
        outputs, gsecond, grads, gnorm_e = feed(
            second, cotangent.reshape(count, dim), norms, perm, weights
        )
    gfirst, gatt_tok, grads, gnorm_c = cross_backward(
        spans,
        each,
        lines if planar else 0,
        live,
        gsecond,
        first,
        norms,
        perm,
        perm_att,
        att_p,
        hid_p,
        cross_q,
        near_p,
        near_kv,
        co_p,
        weights,
        grads,
    )
    if planar:
        others = jnp.concatenate(
            [jnp.zeros((2, dim), f32), gnorm_c, gnorm_e, jnp.zeros((2, dim), f32)], axis=0
        )
        grads, grad_inputs, norm_grads = finish(
            pairs,
            lines,
            qkv,
            att,
            gatt_tok,
            lse,
            hid,
            x,
            gfirst,
            norms,
            perm,
            others,
            weights,
            grads,
        )
        grad_shard, norm_sums = reduce_grads(lines, grads, norm_grads)
        norm_shard = lax.dynamic_slice(norm_sums, (0, lax.axis_index("dp") * part), (6, part))
    else:
        gatt = lax.all_to_all(
            gatt_tok.reshape(seqs, tokens, shares, width)
            .transpose(0, 2, 1, 3)
            .reshape(devices, tokens, width),
            "seq",
            0,
            0,
        ).reshape(length, width)
        gqkv, ghid = self_backward(pairs, qkv, att, gatt, lse, hid, w_qkv)
        parts = (
            lax.all_to_all(ghid.reshape(devices, tokens, dim), "seq", 0, 0)
            .reshape(seqs, shares, tokens, dim)
            .transpose(1, 0, 2, 3)
            .reshape(shares, count, dim)
        )
        grad_inputs, gnorm_a = last_norm(parts, x, gfirst, norms, perm)
        gqkv = gqkv.reshape(dim, 3, 1, width)[..., : held * HEAD]
        gqkv = jnp.where(jnp.arange(shares)[:, None] == share, gqkv, jnp.zeros_like(gqkv))
        grads = lax.dynamic_update_slice(grads, gqkv.reshape(dim, 3 * dim), (0, 0))
        norm_grads = lax.psum(jnp.concatenate([gnorm_a, gnorm_c, gnorm_e], axis=0), "seq")
        partial_sum = lax.psum_scatter(grads, "seq", scatter_dimension=1, tiled=True)
        grad_shard = lax.psum_scatter(partial_sum, "dp", scatter_dimension=0, tiled=True)
        grad_shard = grad_shard.astype(f32)
        norm_shard = lax.psum_scatter(
            norm_grads.astype(bf16), "dp", scatter_dimension=1, tiled=True
        ).astype(f32)
    w_first_new, w_second_new, w_new, w_average_new = adam_update(
        grad_shard, w_master, w_first, w_second, w_average, learn_rate, weight_decay
    )
    n_first_new, n_second_new, n_new, n_average_new = adam_update(
        norm_shard, n_master, n_first, n_second, n_average, norm_rate, 0.0
    )
    return (
        outputs.reshape(seqs, tokens, dim),
        grad_inputs.reshape(seqs, tokens, dim),
        w_first_new,
        w_second_new,
        w_new,
        w_average_new,
        n_first_new,
        n_second_new,
        n_new,
        n_average_new,
    )


def solution(mesh):
    in_specs = (
        P("dp", "seq", None),
        P("dp", "seq", None),
        P("dp", "seq", None, None, None),
        P("dp", "seq", None),
        P(),
        P("dp", "seq"),
        P("dp", "seq"),
        P("dp", "seq"),
        P("dp", "seq"),
        P(None, "dp"),
        P(None, "dp"),
        P(None, "dp"),
        P(None, "dp"),
    )
    out_specs = (
        P("dp", "seq", None),
        P("dp", "seq", None),
        P("dp", "seq"),
        P("dp", "seq"),
        P("dp", "seq"),
        P("dp", "seq"),
        P(None, "dp"),
        P(None, "dp"),
        P(None, "dp"),
        P(None, "dp"),
    )
    return jax.shard_map(
        on_device, mesh=mesh, in_specs=in_specs, out_specs=out_specs, check_vma=False
    )
```

profile of v0, /device:TPU:0, one launch (start us, length us, event | category | flops | bytes accessed | tf_op | source)
XLA Modules:
  0.0 334.1 jit_solution(6627231558000857821)
XLA Ops:
  0.6 0.0 copy-start.9
  0.7 0.0 copy-start.4
  0.7 2.1 fusion.perm_ref.perm_att_ref
  2.8 0.0 copy-done.9
  2.8 0.1 copy.26
  2.9 0.6 reshape.39.presence_ref
  3.5 0.0 copy-done.4
  3.5 0.6 pad.4.norm_ref
  4.1 148.1 %forward.1 = (bf16[768,12288]{1,0:T(8,128)(2,1)}, bf16[768,12288]{1,0:T(8,128)(2,1)}, bf16[1024,768]{1,0:T(8,128)(2,1)}, bf16[9,1024,128]{2,1,0:T(8,128)(2,1)}, ...) custom-call(s32[16]{0:T(128)} %reshape.39.presence_ref, ...), custom_call_target="tpu_custom_call" | custom-call | tf_op jit(solution)/shard_map/forward/pallas_call | solution.py:1426
  152.3 0.0 copy-start.8
  152.3 39.0 %cross_backward.1 = (f32[512,768]{1,0:T(8,128)}, bf16[1024,384]{1,0:T(8,128)(2,1)}, bf16[768,12288]{1,0:T(8,128)(2,1)}, f32[2,768]{1,0:T(2,128)}) custom-call(s32[16]{0:T(128)} %reshape.39.presence_ref, f32[512,768]{1,0:T(8,128)} %get-tuple-element.39.gsecond_ref, f32[512,768]{1,0:T(8,128)} %get-tuple-element.40.first_ref, ...), custom_call_target="tpu_custom_call", output_to_operand_aliasing={{2}: (15, {})} | custom-call | tf_op jit(solution)/shard_map/cross_backward/pallas_call | solution.py:1002
  191.3 0.0 copy-done.8
  191.3 1.3 pad_maximum_fusion.others_ref
  192.6 43.9 %finish.1 = (bf16[768,12288]{1,0:T(8,128)(2,1)}, f32[512,768]{1,0:T(8,128)}, f32[8,768]{1,0:T(8,128)}) custom-call(bf16[9,1024,128]{2,1,0:T(8,128)(2,1)} %get-tuple-element.37.qkv_ref, bf16[1024,384]{1,0:T(8,128)(2,1)} %get-tuple-element.38.att_ref, bf16[1024,384]{1,0:T(8,128)(2,1)} %get-tuple-element.50.gatt_ref, ...), custom_call_target="tpu_custom_call", output_to_operand_aliasing={{0}: (11, {})} | custom-call | tf_op jit(solution)/shard_map/finish/pallas_call | solution.py:526
  236.5 0.0 copy-start
  236.5 0.0 copy-start.2
  236.5 0.0 copy-start.3
  236.6 87.8 %reduce_grads.1 = (f32[192,1536]{1,0:T(8,128)}, f32[8,768]{1,0:T(8,128)}) custom-call(bf16[768,12288]{1,0:T(8,128)(2,1)} %get-tuple-element.58.grads_ref, f32[8,768]{1,0:T(8,128)} %get-tuple-element.59.small_ref), custom_call_target="tpu_custom_call" | custom-call | tf_op jit(solution)/shard_map/reduce_grads/pallas_call | solution.py:1670
  324.3 0.0 copy-done
  324.3 0.0 copy-done.2
  324.3 0.0 copy-done.3
  324.3 0.0 copy-start.5
  324.4 0.0 copy-start.6
  324.4 0.0 copy-start.7
  324.4 4.5 %add_multiply_fusion = (f32[192,1536]{1,0:T(8,128)}, f32[192,1536]{1,0:T(8,128)}, f32[192,1536]{1,0:T(8,128)}, f32[192,1536]{1,0:T(8,128)}) fusion(f32[192,1536]{1,0:T(8,128)S(1)} %copy-done.2, f32[192,1536]{1,0:T(8,128)S(1)} %copy-done, f32[192,1536]{1,0:T(8,128)} %get-tuple-element.60, f32[192,1536]{1,0:T(8,128)S(1)} %copy-done.3, f32[192,1536]{1,0:T(8,128)} %param.19), kind=kLoop, calls=%fused_computation.4 | loop fusion | flops 5013504 | bytes 10616832 | tf_op jit(solution)/shard_map/add | solution.py:1716
  328.9 0.0 copy-done.5
  328.9 0.0 copy-done.6
  328.9 0.0 copy-done.7
  328.9 1.5 add_multiply_fusion.1
  330.4 2.1 copy.31
  332.5 0.0 copy-done.1
  332.5 1.1 copy.32
  (3 shorter events, 0.0 us)
Async XLA Ops:
  0.6 2.1 copy-start.9
  0.7 2.8 copy-start.4
  152.3 39.1 %copy-start.8 = (f32[2,768]{1,0:T(2,128)S(1)}, f32[2,768]{1,0:T(2,128)}, u32[]{:S(2)}) copy-start(f32[2,768]{1,0:T(2,128)} %get-tuple-element.55) | copy-start | bytes 18436
  236.5 87.8 %copy-start = (f32[192,1536]{1,0:T(8,128)S(1)}, f32[192,1536]{1,0:T(8,128)}, u32[]{:S(2)}) copy-start(f32[192,1536]{1,0:T(8,128)} %w_ref.1) | copy-start | bytes 3538948
  236.5 87.8 %copy-start.2 = (f32[192,1536]{1,0:T(8,128)S(1)}, f32[192,1536]{1,0:T(8,128)}, u32[]{:S(2)}) copy-start(f32[192,1536]{1,0:T(8,128)} %param.21) | copy-start | bytes 3538948
  236.5 87.8 %copy-start.3 = (f32[192,1536]{1,0:T(8,128)S(1)}, f32[192,1536]{1,0:T(8,128)}, u32[]{:S(2)}) copy-start(f32[192,1536]{1,0:T(8,128)} %param.20) | copy-start | bytes 3538948
  324.3 4.5 %copy-start.5 = (f32[6,192]{1,0:T(8,128)S(1)}, f32[6,192]{1,0:T(8,128)}, u32[]{:S(2)}) copy-start(f32[6,192]{1,0:T(8,128)} %param.25) | copy-start | bytes 13828
  324.4 4.5 %copy-start.6 = (f32[6,192]{1,0:T(8,128)S(1)}, f32[6,192]{1,0:T(8,128)}, u32[]{:S(2)}) copy-start(f32[6,192]{1,0:T(8,128)} %param.24) | copy-start | bytes 13828
  324.4 4.5 %copy-start.7 = (f32[6,192]{1,0:T(8,128)S(1)}, f32[6,192]{1,0:T(8,128)}, u32[]{:S(2)}) copy-start(f32[6,192]{1,0:T(8,128)} %param.23) | copy-start | bytes 13828
  328.9 3.6 %copy-start.1 = (f32[512,768]{1,0:T(8,128)S(1)}, f32[512,768]{1,0:T(8,128)}, u32[]{:S(2)}) copy-start(f32[512,768]{1,0:T(8,128)} %get-tuple-element.57) | copy-start | bytes 4718596
where the time goes:
time: 337 us; the launch traced here: 334 us
  Pallas kernels  319 us (95%)
  other arithmetic  9.47 us (3%)
  local copies, waits for them, and re-layouts  4.57 us (1%)
    pallas_call x1, Pallas kernels, forward(): pl.pallas_call(partial(forward_kernel, lines, pairs, spans, neighbours),...  148 us
    pallas_call x1, Pallas kernels, reduce_grads(): pl.pallas_call(partial(reduce_kernel, lines), out_shape=(jax.ShapeDtypeSt...  87.8 us
    pallas_call x1, Pallas kernels, finish(): pl.pallas_call(partial(finish_kernel, pairs, lines), out_shape=(jax.Shape...  43.9 us
    pallas_call x1, Pallas kernels, cross_backward(): pl.pallas_call(partial(cross_backward_kernel, spans, neighbours, lines),...  39 us

commit v1 on v0

--- a/solution.py
+++ b/solution.py
@@ -21,7 +21,7 @@
 ema_decay = 0.5
 norm_eps = 1e-05
 masked_score = -1e30
-VMEM_BYTES = 60 * 1024 * 1024
+VMEM_BYTES = 62 * 1024 * 1024
 bf16 = jnp.bfloat16
 f32 = jnp.float32
 
@@ -142,7 +142,7 @@
 
 class Sender:
     def __init__(self, place, send_sems):
-        self.place, self.sems, self.open = place, send_sems, []
+        self.place, self.sems, self.open, self.count = place, send_sems, [], 0
 
     def start(self, condition, src, dst, recv_sem, z=None, seq=None):
         place = self.place
@@ -150,12 +150,13 @@
         copy = pltpu.make_async_remote_copy(
             src_ref=src,
             dst_ref=dst,
-            send_sem=self.sems.at[len(self.open)],
+            send_sem=self.sems.at[self.count],
             recv_sem=recv_sem,
             device_id=target,
             device_id_type=MESH,
         )
         self.open.append((condition, copy))
+        self.count += 1
         when(condition, copy.start)
 
     def arrived(self, condition, ref, recv_sem):
@@ -172,6 +173,7 @@
     def finish(self):
         for condition, copy in self.open:
             when(condition, copy.wait_send)
+        self.open = []
 
 
 class Weave:
@@ -390,169 +392,6 @@
     )(qkv, att, gatt, lse, hid, w)
 
 
-def finish_kernel(
-    pairs,
-    lines,
-    qkv_ref,
-    att_ref,
-    gatt_ref,
-    lse_ref,
-    hid_ref,
-    x_ref,
-    gfirst_ref,
-    norms_ref,
-    perm_ref,
-    others_ref,
-    wts_ref,
-    _,
-    all_ref,
-    gin_ref,
-    small_ref,
-    grad_ref,
-    acc_ref,
-    gw_ref,
-    w_ref,
-    sems,
-    ghid_ref,
-    gsib_ref,
-    parts_ref,
-    gsib_sems,
-    part_sems,
-    send_sems,
-):
-    length, dim = hid_ref.shape
-    width = pairs * LANES
-    tokens = length // 8
-    place = Place(lines)
-    me, core = place.me, place.core
-    place.meet()
-    send = Sender(place, send_sems)
-    copies = weight_copies(pairs, dim, wts_ref, w_ref, sems)
-    for copy in copies:
-        copy.start()
-
-    share_count = dim // width
-    share = lax.rem(me, share_count)
-    gw_ref[3] = jnp.zeros_like(gw_ref[3])
-    outs = []
-    for part in range(3):
-        for other in range(1, share_count):
-            first = part * dim + lax.rem(share + other, share_count) * width
-            outs.append(
-                pltpu.make_async_copy(
-                    gw_ref.at[3],
-                    all_ref.at[:, pl.ds(pl.multiple_of(first, LANES), width)],
-                    sems.at[6 + part * (share_count - 1) + other - 1],
-                )
-            )
-            outs[-1].start()
-
-    attention = (qkv_ref, att_ref, gatt_ref, lse_ref, grad_ref, acc_ref)
-
-    @pl.loop(0, pairs)
-    def _(pair):
-        pair_backward(pair, pairs, *attention, lambda: None)
-
-    def token_rows(device):
-        return pl.ds(pl.multiple_of(device * tokens, tokens), tokens)
-
-    for copy in copies:
-        copy.wait()
-    for begin in range(0, length, 256):
-        rows = slice(begin, begin + 256)
-        ghid_ref[rows, :] = nt(grad_ref[rows, :], w_ref[...]).astype(bf16)
-    chips = (place.xn // 2, place.yn // 2, place.dg // 2, place.chip)
-    for chip in chips:
-        theirs = chip * 2 + 1 - core
-        send.start(
-            None, ghid_ref.at[token_rows(theirs)], gsib_ref.at[chip], gsib_sems.at[chip], seq=place.sib
-        )
-    for chip in chips:
-        send.arrived(None, gsib_ref.at[chip], gsib_sems.at[chip])
-        rows = token_rows(chip * 2 + core)
-        total = (ghid_ref[rows, :].astype(f32) + gsib_ref[chip].astype(f32)).astype(bf16)
-        if chip is place.chip:
-            parts_ref[chip] = total
-        else:
-            ghid_ref[rows, :] = total
-            send.start(
-                None,
-                ghid_ref.at[rows],
-                parts_ref.at[place.chip],
-                part_sems.at[place.chip],
-                seq=chip * 2 + core,
-            )
-
-    hidden_t = hid_ref[...].T
-    for part in range(3):
-        gw_ref[part] = mm(hidden_t, grad_ref[:, part * width : (part + 1) * width]).astype(bf16)
-        first = part * dim + share * width
-        outs.append(
-            pltpu.make_async_copy(
-                gw_ref.at[part],
-                all_ref.at[:, pl.ds(pl.multiple_of(first, LANES), width)],
-                sems.at[3 + part],
-            )
-        )
-        outs[-1].start()
-
-    for chip in chips[:3]:
-        send.arrived(None, parts_ref.at[chip], part_sems.at[chip])
-    gain_sum = shift_sum = None
-    for chip in range(4):
-        rows = slice(chip * tokens, (chip + 1) * tokens)
-        upstream = nt(parts_ref[chip], perm_ref[...])
-        normed, recip = centre_scale(x_ref[rows, :].astype(f32))
-        back, gain, shift = norm_back(upstream, normed, recip, norms_ref[0:1, :])
-        gin_ref[rows, :] = gfirst_ref[rows, :] + back
-        gain_sum = gain if gain_sum is None else gain_sum + gain
-        shift_sum = shift if shift_sum is None else shift_sum + shift
-    small_ref[...] = others_ref[...]
-    small_ref[0:1, :] = gain_sum
-    small_ref[1:2, :] = shift_sum
-    for copy in outs:
-        copy.wait()
-    send.finish()
-
-
-def finish(pairs, lines, qkv, att, gatt, lse, hid, x, gfirst, norms, perm, others, weights, grads):
-    length, dim = hid.shape
-    width = pairs * LANES
-    count = x.shape[0]
-    tokens = length // 8
-    any_space = pl.BlockSpec(memory_space=pl.ANY)
-    vmem = pl.BlockSpec(memory_space=pltpu.VMEM)
-    dma = pltpu.SemaphoreType.DMA
-    return pl.pallas_call(
-        partial(finish_kernel, pairs, lines),
-        out_shape=(
-            jax.ShapeDtypeStruct(grads.shape, bf16),
-            jax.ShapeDtypeStruct((count, dim), f32),
-            jax.ShapeDtypeStruct((8, dim), f32),
-        ),
-        in_specs=[vmem] * 10 + [any_space] * 2,
-        out_specs=(any_space, vmem, vmem),
-        scratch_shapes=[
-            pltpu.VMEM((length, 3 * width), bf16),
-            pltpu.VMEM((2, length, LANES), f32),
-            pltpu.VMEM((4, dim, width), bf16),
-            pltpu.VMEM((dim, 3 * width), bf16),
-            dma((6 + 3 * (dim // width),)),
-            pltpu.VMEM((length, dim), bf16),
-            pltpu.VMEM((4, tokens, dim), bf16),
-            pltpu.VMEM((4, tokens, dim), bf16),
-            dma((4,)),
-            dma((4,)),
-            dma((8,)),
-        ],
-        input_output_aliases={11: 0},
-        compiler_params=pltpu.CompilerParams(
-            vmem_limit_bytes=VMEM_BYTES, collective_id=3, has_side_effects=True
-        ),
-        name="finish",
-    )(qkv, att, gatt, lse, hid, x, gfirst, norms, perm, others, weights, grads)
-
-
 def spread_heads(block, rows, group):
     lane = lax.broadcasted_iota(jnp.int32, block.shape, 1) // HEAD
     return jnp.concatenate([pick(lane == head, block) for head in range(group)], axis=0)
@@ -814,10 +653,40 @@
     )(*operands, weights, weights)
 
 
+def span_backward(
+    span, spans, neighbours, presence_ref, cross_q_ref, gco_ref, near_kv_ref, gcq_ref, gnear_ref
+):
+    count, dim = cross_q_ref.shape
+    span_len = count // spans
+    near = near_kv_ref.shape[0] // spans
+    group = 256 // HEAD
+    rows = rows_of(span, span_len)
+    keys = rows_of(span, near)
+    live, anyone = live_keys(presence_ref, span, (near, 1), 0, neighbours, near // neighbours)
+    for begin in range(0, dim, group * HEAD):
+        lanes = slice(begin, begin + group * HEAD)
+        lanes_v = slice(dim + begin, dim + begin + group * HEAD)
+        query = spread_heads(cross_q_ref[rows, lanes] * SCALE, span_len, group)
+        grad_out = spread_heads(gco_ref[rows, lanes], span_len, group)
+        key = near_kv_ref[keys, lanes]
+        scores = jnp.where(live > 0, nt(key, query), masked_score)
+        peak = jnp.max(scores, axis=0, keepdims=True)
+        expon = jnp.exp(scores - peak) * live
+        total = jnp.sum(expon, axis=0, keepdims=True) + 1.0 - anyone
+        probs = expon * (1.0 / total)
+        grad_probs = nt(near_kv_ref[keys, lanes_v], grad_out)
+        inner = jnp.sum(probs * grad_probs, axis=0, keepdims=True)
+        grad_scores = (probs * (grad_probs - inner)).astype(bf16)
+        gcq_ref[rows, lanes] = (
+            gather_heads(tn(grad_scores, key), span_len, group) * SCALE
+        ).astype(bf16)
+        gnear_ref[keys, lanes] = mm(grad_scores, query).astype(bf16)
+        gnear_ref[keys, lanes_v] = mm(probs.astype(bf16), grad_out).astype(bf16)
+
+
 def cross_backward_kernel(
     spans,
     neighbours,
-    lines,
     presence_ref,
     gsecond_ref,
     first_ref,
@@ -838,64 +707,28 @@
     gatt_ref,
     all_ref,
     gnorm_ref,
-    *rest,
+    gco_ref,
+    gcq_ref,
+    gnear_ref,
+    gw_ref,
+    sems,
 ):
-    count, dim = first_ref.shape
-    rows_near = near_p_ref.shape[0]
-    span_len = count // spans
-    near = rows_near // spans
-    group = 256 // HEAD
+    dim = first_ref.shape[1]
     outs = []
-    if lines:
-        gatt_tok_ref, row_sems, send_sems = rest[5:]
-        place = Place(lines)
-        place.meet()
-        send = Sender(place, send_sems)
-    gco_ref, gcq_ref, gnear_ref, gw_ref, sems = rest[:5]
 
     def keep(index, value):
-        slot = len(outs) % 3
-        if len(outs) >= 3:
-            outs[-3].wait()
-        gw_ref[slot] = value.astype(bf16)
+        gw_ref[index] = value.astype(bf16)
         outs.append(
             pltpu.make_async_copy(
-                gw_ref.at[slot],
-                all_ref.at[:, pl.ds((3 + index) * dim, dim)],
-                sems.at[index],
+                gw_ref.at[index], all_ref.at[:, pl.ds((3 + index) * dim, dim)], sems.at[index]
             )
         )
         outs[-1].start()
 
     upper = gsecond_ref[...].astype(bf16)
     gco_ref[...] = nt(nt(upper, w_co_ref[...]).astype(bf16), perm_ref[...]).astype(bf16)
-
-    def one_span(span):
-        rows = rows_of(span, span_len)
-        keys = rows_of(span, near)
-        live, anyone = live_keys(presence_ref, span, (near, 1), 0, neighbours, near // neighbours)
-        for begin in range(0, dim, group * HEAD):
-            lanes = slice(begin, begin + group * HEAD)
-            lanes_v = slice(dim + begin, dim + begin + group * HEAD)
-            query = spread_heads(cross_q_ref[rows, lanes] * SCALE, span_len, group)
-            grad_out = spread_heads(gco_ref[rows, lanes], span_len, group)
-            key = near_kv_ref[keys, lanes]
-            scores = jnp.where(live > 0, nt(key, query), masked_score)
-            peak = jnp.max(scores, axis=0, keepdims=True)
-            expon = jnp.exp(scores - peak) * live
-            total = jnp.sum(expon, axis=0, keepdims=True) + 1.0 - anyone
-            probs = expon * (1.0 / total)
-            grad_probs = nt(near_kv_ref[keys, lanes_v], grad_out)
-            inner = jnp.sum(probs * grad_probs, axis=0, keepdims=True)
-            grad_scores = (probs * (grad_probs - inner)).astype(bf16)
-            gcq_ref[rows, lanes] = (
-                gather_heads(tn(grad_scores, key), span_len, group) * SCALE
-            ).astype(bf16)
-            gnear_ref[keys, lanes] = mm(grad_scores, query).astype(bf16)
-            gnear_ref[keys, lanes_v] = mm(probs.astype(bf16), grad_out).astype(bf16)
-
-    pl.loop(0, spans)(one_span)
-
+    tables = (presence_ref, cross_q_ref, gco_ref, near_kv_ref, gcq_ref, gnear_ref)
+    pl.loop(0, spans)(lambda span: span_backward(span, spans, neighbours, *tables))
     upstream = nt(nt(gcq_ref[...], w_cq_ref[...]).astype(bf16), perm_ref[...])
     normed, recip = centre_scale(first_ref[...])
     back, gain, shift = norm_back(upstream, normed, recip, norms_ref[2:3, :])
@@ -903,47 +736,20 @@
     gnorm_ref[1:2, :] = shift
     gfirst_ref[...] = gsecond_ref[...] + back
     lower = gfirst_ref[...].astype(bf16)
-    gatt = nt(nt(lower, w_out_ref[...]).astype(bf16), perm_att_ref[...]).astype(bf16)
-    if lines:
-        width = gatt_ref.shape[1]
-        tokens = gatt_ref.shape[0] // 8
-        shares = gatt.shape[1] // width
-        gatt_tok_ref[...] = gatt
-
-        def block(device):
-            return gatt_tok_ref.at[
-                pl.ds(pl.multiple_of(device // shares * tokens, tokens), tokens),
-                pl.ds(pl.multiple_of(device % shares * width, width), width),
-            ]
-
-        def landing(device):
-            return gatt_ref.at[pl.ds(pl.multiple_of(device * tokens, tokens), tokens)]
-
-        for other in place.plane():
-            send.start(None, block(other), landing(place.me), row_sems.at[place.me], seq=other)
-        own = pltpu.make_async_copy(block(place.me), landing(place.me), row_sems.at[place.me])
-        own.start()
-    else:
-        gatt_ref[...] = gatt
+    gatt_ref[...] = nt(nt(lower, w_out_ref[...]).astype(bf16), perm_att_ref[...]).astype(bf16)
     keep(4, mm(co_p_ref[...].T, upper))
     near_t = near_p_ref[...].T
     for part in range(2):
         keep(2 + part, mm(near_t, gnear_ref[:, part * dim : (part + 1) * dim]))
     keep(1, mm(hid_p_ref[...].T, gcq_ref[...]))
     keep(0, mm(att_p_ref[...].T, lower))
-    if lines:
-        for other in place.plane():
-            send.arrived(None, landing(other), row_sems.at[other])
-        own.wait()
-        send.finish()
-    for copy in outs[-3:]:
+    for copy in outs:
         copy.wait()
 
 
 def cross_backward(
     spans,
     neighbours,
-    lines,
     presence,
     gsecond,
     first,
@@ -961,10 +767,9 @@
 ):
     count, dim = first.shape
     rows_near = near_p.shape[0]
-    gatt_shape = (count, perm_att.shape[0])
     out_shape = [
         jax.ShapeDtypeStruct((count, dim), f32),
-        jax.ShapeDtypeStruct(gatt_shape, bf16),
+        jax.ShapeDtypeStruct((count, perm_att.shape[0]), bf16),
         jax.ShapeDtypeStruct(grads.shape, bf16),
         jax.ShapeDtypeStruct((2, dim), f32),
     ]
@@ -972,20 +777,9 @@
         pltpu.VMEM((count, dim), bf16),
         pltpu.VMEM((count, dim), bf16),
         pltpu.VMEM((rows_near, 2 * dim), bf16),
-        pltpu.VMEM((3, dim, dim), bf16),
+        pltpu.VMEM((5, dim, dim), bf16),
         pltpu.SemaphoreType.DMA((5,)),
     ]
-    compiler_params = params()
-    if lines:
-        out_shape[1] = jax.ShapeDtypeStruct((2 * count, gatt_shape[1] // 2), bf16)
-        scratch += [
-            pltpu.VMEM(gatt_shape, bf16),
-            pltpu.SemaphoreType.DMA((8,)),
-            pltpu.SemaphoreType.DMA((8,)),
-        ]
-        compiler_params = pltpu.CompilerParams(
-            vmem_limit_bytes=VMEM_BYTES, collective_id=2, has_side_effects=True
-        )
     operands = (
         gsecond,
         first,
@@ -1000,7 +794,7 @@
         co_p,
     )
     return pl.pallas_call(
-        partial(cross_backward_kernel, spans, neighbours, lines),
+        partial(cross_backward_kernel, spans, neighbours),
         out_shape=out_shape,
         grid=(1,),
         in_specs=[pl.BlockSpec(memory_space=pltpu.SMEM)]
@@ -1013,7 +807,7 @@
         ),
         scratch_shapes=scratch,
         input_output_aliases={len(operands) + 4: 2},
-        compiler_params=compiler_params,
+        compiler_params=params(),
         name="cross_backward",
     )(presence, *operands, *([weights] * 3), grads)
 
@@ -1043,7 +837,7 @@
     )(parts, x, gfirst, norms, perm)
 
 
-def forward_kernel(
+def layer_kernel(
     lines,
     pairs,
     spans,
@@ -1052,77 +846,64 @@
     w_ref,
     norm_ref,
     x_ref,
-    perm_ref,
+    order_ref,
     cot_ref,
     near_ref,
     wts_ref,
     all_ref,
-    hid_out,
-    qkv_out,
-    att_out,
-    lse_out,
-    att_p_out,
-    first_out,
-    hid_p_out,
-    cross_q_out,
-    near_p_out,
-    near_kv_out,
-    co_p_out,
+    out_ref,
+    gin_ref,
+    sums_ref,
+    hid_ref,
+    qkv_ref,
+    att_ref,
+    lse_ref,
+    att_p_ref,
+    first_ref,
+    hid_p_ref,
+    cross_q_ref,
+    near_p_ref,
+    near_kv_ref,
+    co_p_ref,
+    second_ref,
+    own_ref,
+    small_ref,
+    rows_ref,
+    w_qkv_ref,
+    w_mid_ref,
+    att_tok_ref,
+    cross_ref,
+    up_p_ref,
+    up_t_ref,
+    cot_p_ref,
+    cot_t_ref,
+    result_ref,
+    back_ref,
+    gfeed_ref,
+    perm_ref,
     norms_ref,
-    out_ref,
-    gsecond_ref,
-    gnorm_ref,
-    *scratch,
+    gatt_ref,
+    acc_ref,
+    gsib_ref,
+    parts_ref,
+    send_sems,
+    z_sems,
+    y_sems,
+    x_sems,
+    a_sems,
+    b_sems,
+    sib_sems,
+    norm_sems,
+    row_sems,
+    att_sems,
+    local_sems,
+    qkv_sems,
+    mid_sems,
+    feed_sems,
+    gatt_sems,
+    gsib_sems,
+    part_sems,
 ):
-    results, scratch = scratch[:11], scratch[11:]
-    (
-        hid_ref,
-        qkv_ref,
-        att_ref,
-        lse_ref,
-        att_p_ref,
-        first_ref,
-        hid_p_ref,
-        cross_q_ref,
-        near_p_ref,
-        near_kv_ref,
-        co_p_ref,
-    ) = results
-    work, scratch = scratch[:15], scratch[15:]
-    (
-        second_ref,
-        own_ref,
-        small_ref,
-        rows_ref,
-        w_qkv_ref,
-        w_mid_ref,
-        att_tok_ref,
-        cross_ref,
-        up_p_ref,
-        up_t_ref,
-        cot_p_ref,
-        cot_t_ref,
-        result_ref,
-        back_ref,
-        gfeed_ref,
-    ) = work
-    (
-        send_sems,
-        z_sems,
-        y_sems,
-        x_sems,
-        a_sems,
-        b_sems,
-        sib_sems,
-        norm_sems,
-        row_sems,
-        att_sems,
-        local_sems,
-        qkv_sems,
-        mid_sems,
-        feed_sems,
-        out_sems,
-    ) = scratch
     place = Place(lines)
     z, me, core = place.z, place.me, place.core
     length, dim = hid_ref.shape
@@ -1139,6 +920,10 @@
     keep = pltpu.make_async_copy(own_ref, unit(z, me), local_sems.at[0])
     keep.start()
 
+    def build_perm():
+        row = lax.broadcasted_iota(jnp.int32, (dim, dim), 0)
+        perm_ref[...] = jnp.where(row == order_ref[0:1, :], 1.0, 0.0).astype(bf16)
+
     def obtain(index):
         condition, line, far, side = events[index]
         mine = unit(line, me)
@@ -1172,25 +957,6 @@
             send.arrived(condition, part, sems.at[line])
             send.start(condition, part, part, sib_sems.at[group, line], seq=place.sib)
 
-    kept = []
-
-    def emit(index):
-        out = (
-            hid_out,
-            qkv_out,
-            att_out,
-            lse_out,
-            att_p_out,
-            first_out,
-            hid_p_out,
-            cross_q_out,
-            near_p_out,
-            near_kv_out,
-            co_p_out,
-        )[index]
-        kept.append(pltpu.make_async_copy(results[index], out, out_sems.at[index]))
-        kept[-1].start()
-
     def row_block(seq):
         return rows_ref.at[pl.ds(pl.multiple_of(seq * tokens, tokens), tokens)]
 
@@ -1209,6 +975,7 @@
     send.start(None, x_ref.at[place.chip], row_block(me), row_sems.at[me], seq=place.sib)
     for other in others:
         send.start(None, x_ref.at[other // 2], row_block(me), row_sems.at[me], seq=other)
+    build_perm()
     near_load.wait()
 
     @pl.loop(0, near_p_ref.shape[0] // 512)
@@ -1216,7 +983,6 @@
         rows = rows_of(step, 512)
         near_p_ref[rows, :] = mm(near_p_ref[rows, :], perm_ref[...]).astype(bf16)
 
-    emit(8)
     obtain(1)
     obtain(2)
     pass_on(0)
@@ -1255,7 +1021,6 @@
             send.arrived(None, row_block(place.sib), row_sems.at[place.sib])
             own_rows.wait()
             norm_rows(rows_ref, norms_ref[...], perm_ref, hid_ref)
-            emit(0)
         pass_on(index - 2)
         pass_on(index - 1)
         corner(index - 4)
@@ -1278,7 +1043,6 @@
     for part in range(3):
         copies[part].wait()
         triple_part(part, pairs, hid_ref, w_qkv_ref, qkv_ref)
-    emit(1)
 
     share = lax.rem(me, dim // width)
     seq_rows = pl.ds(pl.multiple_of(place.chip * tokens, tokens), tokens)
@@ -1296,8 +1060,6 @@
             send.start(None, block, to, att_sems.at[pair, me], seq=other)
         own_block = att_ref[pl.ds(pl.multiple_of(me * tokens, tokens), tokens), lanes]
         landing(pair, seq_rows, share)[...] = own_block
-    emit(2)
-    emit(3)
 
     for index in (2, 3, 0, 1, 4):
         middle(index).wait()
@@ -1305,23 +1067,18 @@
         rows = slice(step * 512, (step + 1) * 512)
         near_kv_ref[rows, :dim] = mm(near_p_ref[rows, :], w_mid_ref[2]).astype(bf16)
         near_kv_ref[rows, dim:] = mm(near_p_ref[rows, :], w_mid_ref[3]).astype(bf16)
-    emit(9)
     w_out_ref, w_cq_ref, w_co_ref = (w_mid_ref.at[index] for index in (0, 1, 4))
     for pair in range(pairs):
         for other in place.plane():
             rows = pl.ds(pl.multiple_of(other // 2 * tokens, tokens), tokens)
             send.arrived(None, landing(pair, rows, lax.rem(other, 2)), att_sems.at[pair, other])
     att_p_ref[...] = mm(att_tok_ref[...], perm_ref[...]).astype(bf16)
-    emit(4)
     own_x = x_ref[...].reshape(first_ref.shape).astype(f32)
     first_ref[...] = own_x + mm(att_p_ref[...], w_out_ref[...])
-    emit(5)
     normed, _ = centre_scale(first_ref[...])
     hidden = (normed * norms_ref[2:3, :] + norms_ref[3:4, :]).astype(bf16)
     hid_p_ref[...] = mm(hidden, perm_ref[...]).astype(bf16)
-    emit(6)
     cross_q_ref[...] = mm(hid_p_ref[...], w_cq_ref[...]).astype(bf16)
-    emit(7)
     pl.loop(0, spans)(
         lambda span: span_forward(
             span, spans, neighbours, presence_ref, cross_q_ref, near_kv_ref, cross_ref
@@ -1355,7 +1112,6 @@
     for copy in tile_load(0) + tile_load(1):
         copy.start()
     co_p_ref[...] = mm(cross_ref[...], perm_ref[...]).astype(bf16)
-    emit(10)
     second_ref[...] = first_ref[...] + mm(co_p_ref[...], w_co_ref[...])
     normed, _ = centre_scale(second_ref[...])
     hidden = (normed * norms_ref[4:5, :] + norms_ref[5:6, :]).astype(bf16)
@@ -1383,23 +1139,161 @@
         if index + 2 < len(order):
             for copy in tile_load(index + 2):
                 copy.start()
+        elif index + 2 == len(order):
+            middle(0).start()
+            middle(1).start()
 
     out_ref[...] = (second_ref[...] + nt(result_ref[...].astype(bf16), perm_ref[...])).astype(bf16)
     upstream = nt(back_ref[...].astype(bf16), perm_ref[...])
     normed, recip = centre_scale(second_ref[...])
     back, gain, shift = norm_back(upstream, normed, recip, norms_ref[4:5, :])
+    gsecond_ref = second_ref
     gsecond_ref[...] = cot_ref[...].astype(f32) + back
-    gnorm_ref[0:1, :] = gain
-    gnorm_ref[1:2, :] = shift
+    sums_ref[4:5, :] = gain
+    sums_ref[5:6, :] = shift
+    sums_ref[6:8, :] = jnp.zeros((2, dim), f32)
     for index in range(len(order) - 2, len(order)):
         for copy in tile_store(index):
             copy.wait()
-    for copy in kept:
+
+    gco_ref, gcq_ref, gatt_tok_ref = up_p_ref, cot_p_ref, cross_ref
+    outs = []
+
+    def store(slot, part, first):
+        copy = pltpu.make_async_copy(
+            part, all_ref.at[:, pl.ds(first, part.shape[1])], feed_sems.at[1, slot]
+        )
+        outs.append(copy)
+        copy.start()
+
+    def keep_grad(index, value):
+        slot = len(outs) % 4
+        if len(outs) >= 4:
+            outs[-4].wait()
+        gfeed_ref[slot] = value.astype(bf16)
+        store(slot, gfeed_ref.at[slot], (3 + index) * dim)
+
+    upper = gsecond_ref[...].astype(bf16)
+    gco_ref[...] = nt(nt(upper, w_co_ref[...]).astype(bf16), perm_ref[...]).astype(bf16)
+    tables = (presence_ref, cross_q_ref, gco_ref, near_kv_ref, gcq_ref, near_kv_ref)
+    pl.loop(0, spans)(lambda span: span_backward(span, spans, neighbours, *tables))
+    for index in (0, 1):
+        middle(index).wait()
+    upstream = nt(nt(gcq_ref[...], w_cq_ref[...]).astype(bf16), perm_ref[...])
+    normed, recip = centre_scale(first_ref[...])
+    back, gain, shift = norm_back(upstream, normed, recip, norms_ref[2:3, :])
+    sums_ref[2:3, :] = gain
+    sums_ref[3:4, :] = shift
+    gfirst_ref = gsecond_ref
+    gfirst_ref[...] = gsecond_ref[...] + back
+    lower = gfirst_ref[...].astype(bf16)
+    gatt_tok_ref[...] = nt(nt(lower, w_out_ref[...]).astype(bf16), perm_ref[...]).astype(bf16)
+
+    def gatt_block(device):
+        return gatt_tok_ref.at[
+            pl.ds(pl.multiple_of(device // 2 * tokens, tokens), tokens),
+            pl.ds(pl.multiple_of(lax.rem(device, 2) * width, width), width),
+        ]
+
+    def gatt_rows(device):
+        return gatt_ref.at[pl.ds(pl.multiple_of(device * tokens, tokens), tokens)]
+
+    for other in place.plane():
+        send.start(None, gatt_block(other), gatt_rows(me), gatt_sems.at[me], seq=other)
+    own_gatt = pltpu.make_async_copy(gatt_block(me), gatt_rows(me), gatt_sems.at[me])
+    own_gatt.start()
+    keep_grad(4, mm(co_p_ref[...].T, upper))
+    near_t = near_p_ref[...].T
+    for part in range(2):
+        keep_grad(2 + part, mm(near_t, near_kv_ref[:, part * dim : (part + 1) * dim]))
+    keep_grad(1, mm(hid_p_ref[...].T, gcq_ref[...]))
+    keep_grad(0, mm(att_p_ref[...].T, lower))
+    for other in place.plane():
+        send.arrived(None, gatt_rows(other), gatt_sems.at[other])
+    own_gatt.wait()
+
+    send.finish()
+    grad_ref = near_kv_ref.at[pl.ds(0, length), pl.ds(0, 3 * width)]
+    ghid_ref = rows_ref
+    attention = (qkv_ref, att_ref, gatt_ref, lse_ref, grad_ref, acc_ref)
+    pl.loop(0, pairs)(lambda pair: pair_backward(pair, pairs, *attention, lambda: None))
+    for begin in range(0, length, 256):
+        rows = slice(begin, begin + 256)
+        ghid_ref[rows, :] = nt(grad_ref[rows, :], w_qkv_ref[...]).astype(bf16)
+    chips = (place.xn // 2, place.yn // 2, place.dg // 2, place.chip)
+
+    def token_rows(device):
+        return pl.ds(pl.multiple_of(device * tokens, tokens), tokens)
+
+    for chip in chips:
+        theirs = ghid_ref.at[token_rows(chip * 2 + 1 - core)]
+        send.start(None, theirs, gsib_ref.at[chip], gsib_sems.at[chip], seq=place.sib)
+
+    for copy in outs[-4:]:
         copy.wait()
+    outs.clear()
+    gfeed_ref[3] = jnp.zeros_like(gfeed_ref[3])
+    share_count = dim // width
+    zeros = [
+        pltpu.make_async_copy(
+            gfeed_ref.at[3, :, pl.ds(0, width)],
+            all_ref.at[
+                :,
+                pl.ds(
+                    pl.multiple_of(part * dim + lax.rem(share + other, share_count) * width, LANES),
+                    width,
+                ),
+            ],
+            mid_sems.at[2 + part],
+        )
+        for part in range(3)
+        for other in range(1, share_count)
+    ]
+    for copy in zeros:
+        copy.start()
+    hidden_t = hid_ref[...].T
+
+    def triple_grad(part):
+        columns = slice(part * width, (part + 1) * width)
+        gfeed_ref[part, :, :width] = mm(hidden_t, grad_ref[:, columns]).astype(bf16)
+        first = pl.multiple_of(part * dim + share * width, LANES)
+        store(part, gfeed_ref.at[part, :, pl.ds(0, width)], first)
+
+    triple_grad(0)
+    triple_grad(1)
+    for chip in chips:
+        send.arrived(None, gsib_ref.at[chip], gsib_sems.at[chip])
+        rows = token_rows(chip * 2 + core)
+        total = (ghid_ref[rows, :].astype(f32) + gsib_ref[chip].astype(f32)).astype(bf16)
+        if chip is place.chip:
+            parts_ref[chip] = total
+        else:
+            ghid_ref[rows, :] = total
+            landed, sem = parts_ref.at[place.chip], part_sems.at[place.chip]
+            send.start(None, ghid_ref.at[rows], landed, sem, seq=chip * 2 + core)
+    triple_grad(2)
+    for chip in chips[:3]:
+        send.arrived(None, parts_ref.at[chip], part_sems.at[chip])
+    gain_sum = shift_sum = None
+    for chip in range(4):
+        rows = slice(chip * tokens, (chip + 1) * tokens)
+        upstream = nt(parts_ref[chip], perm_ref[...])
+        normed, recip = centre_scale(x_ref[chip].astype(f32))
+        back, gain, shift = norm_back(upstream, normed, recip, norms_ref[0:1, :])
+        gfirst_ref[rows, :] += back
+        gain_sum = gain if gain_sum is None else gain_sum + gain
+        shift_sum = shift if shift_sum is None else shift_sum + shift
+    leave = pltpu.make_async_copy(gfirst_ref, gin_ref, local_sems.at[0])
+    leave.start()
+    sums_ref[0:1, :] = gain_sum
+    sums_ref[1:2, :] = shift_sum
+    for copy in outs + zeros:
+        copy.wait()
+    leave.wait()
     send.finish()
 
 
-def forward(lines, pairs, spans, neighbours, presence, w_shard, n_shard, inputs, perm, cot, near):
+def layer(lines, pairs, spans, neighbours, presence, w_shard, n_shard, inputs, order, cot, near):
     unit_rows, unit_cols = w_shard.shape
     seqs, tokens, dim = inputs.shape
     count, length, width = seqs * tokens, 8 * tokens, pairs * LANES
@@ -1409,50 +1303,56 @@
     vmem = pl.BlockSpec(memory_space=pltpu.VMEM)
     dma = pltpu.SemaphoreType.DMA
     packed = jax.ShapeDtypeStruct((unit_rows * lines, unit_cols * 8), bf16)
-    kept = (
+    tile = unit_cols // 2
+    tokens_rows = (count, dim)
+    scratch = [
         ((length, dim), bf16),
         ((3 * pairs, length, LANES), bf16),
         ((length, width), bf16),
         ((pairs, 2, length), f32),
-        ((count, dim), bf16),
-        ((count, dim), f32),
-        ((count, dim), bf16),
-        ((count, dim), bf16),
+        (tokens_rows, bf16),
+        (tokens_rows, f32),
+        (tokens_rows, bf16),
+        (tokens_rows, bf16),
         ((rows_near, dim), bf16),
         ((rows_near, 2 * dim), bf16),
-        ((count, dim), bf16),
-    )
-    tile = unit_cols // 2
+        (tokens_rows, bf16),
+        (tokens_rows, f32),
+        ((unit_rows, unit_cols), bf16),
+        ((lines,) + n_shard.shape, bf16),
+        ((length, dim), bf16),
+        ((dim, 3 * width), bf16),
+        ((5, dim, dim), bf16),
+        (tokens_rows, bf16),
+        (tokens_rows, bf16),
+        (tokens_rows, bf16),
+        ((dim, count), bf16),
+        (tokens_rows, bf16),
+        ((dim, count), bf16),
+        (tokens_rows, f32),
+        (tokens_rows, f32),
+        ((4, dim, tile), bf16),
+        ((dim, dim), bf16),
+        ((8, dim), f32),
+        ((length, width), bf16),
+        ((2, length, LANES), f32),
+        ((4, tokens, dim), bf16),
+        ((4, tokens, dim), bf16),
+    ]
     return pl.pallas_call(
-        partial(forward_kernel, lines, pairs, spans, neighbours),
-        out_shape=(packed, packed)
-        + tuple(jax.ShapeDtypeStruct(*entry) for entry in kept)
-        + (
+        partial(layer_kernel, lines, pairs, spans, neighbours),
+        out_shape=(
+            packed,
+            packed,
+            jax.ShapeDtypeStruct(tokens_rows, bf16),
+            jax.ShapeDtypeStruct(tokens_rows, f32),
             jax.ShapeDtypeStruct((8, dim), f32),
-            jax.ShapeDtypeStruct((count, dim), bf16),
-            jax.ShapeDtypeStruct((count, dim), f32),
-            jax.ShapeDtypeStruct((2, dim), f32),
         ),
         in_specs=[pl.BlockSpec(memory_space=pltpu.SMEM)] + [vmem] * 5 + [any_space],
-        out_specs=(any_space,) * (2 + len(kept)) + (vmem,) * 4,
-        scratch_shapes=[pltpu.VMEM(*entry) for entry in kept]
+        out_specs=(any_space, any_space, vmem, any_space, vmem),
+        scratch_shapes=[pltpu.VMEM(*entry) for entry in scratch]
         + [
-            pltpu.VMEM((count, dim), f32),
-            pltpu.VMEM((unit_rows, unit_cols), bf16),
-            pltpu.VMEM((lines,) + n_shard.shape, bf16),
-            pltpu.VMEM((length, dim), bf16),
-            pltpu.VMEM((dim, 3 * width), bf16),
-            pltpu.VMEM((5, dim, dim), bf16),
-            pltpu.VMEM((count, dim), bf16),
-            pltpu.VMEM((count, dim), bf16),
-            pltpu.VMEM((count, dim), bf16),
-            pltpu.VMEM((dim, count), bf16),
-            pltpu.VMEM((count, dim), bf16),
-            pltpu.VMEM((dim, count), bf16),
-            pltpu.VMEM((count, dim), f32),
-            pltpu.VMEM((count, dim), f32),
-            pltpu.VMEM((4, dim, tile), bf16),
-            dma((11 * events + 7 + lines + 7 * pairs,)),
+            dma((11 * events + 7 + lines + 7 * pairs + 16,)),
             dma((lines,)),
             dma((lines,)),
             dma((lines,)),
@@ -1466,13 +1366,15 @@
             dma((3,)),
             dma((5,)),
             dma((2, 4)),
-            dma((len(kept),)),
+            dma((8,)),
+            dma((4,)),
+            dma((4,)),
         ],
         compiler_params=pltpu.CompilerParams(
             vmem_limit_bytes=VMEM_BYTES, collective_id=1, has_side_effects=True
         ),
-        name="forward",
-    )(presence, w_shard, n_shard, inputs, perm, cot, near)
+        name="layer",
+    )(presence, w_shard, n_shard, inputs, order, cot, near)
 
 
 def reduce_kernel(
@@ -1747,12 +1649,8 @@
 
     lines = lax.axis_size("dp")
     planar = devices == 8 and seqs == 4 and spare == 0
-    perm = (jnp.arange(dim)[:, None] == row_order[None, :]).astype(bf16)
-    perm_att = perm
-    if spare:
-        perm_att = jnp.pad(perm.reshape(shares, held * HEAD, dim), ((0, 0), (0, spare), (0, 0)))
-        perm_att = perm_att.reshape(shares * width, dim)
     x = inputs.reshape(count, dim)
+    cot = cotangent.reshape(count, dim)
     spans = seqs * neighbours.shape[1]
     each = neighbours.shape[2]
     near = neighbours.reshape(-1, dim)
@@ -1760,38 +1658,16 @@
     part = n_master.shape[1]
     if planar:
         small = jnp.pad(n_master.astype(bf16), ((0, 16 - 6), (0, -part % LANES)))
-        (
-            weights,
-            grads,
-            hid,
-            qkv,
-            att,
-            lse,
-            att_p,
-            first,
-            hid_p,
-            cross_q,
-            near_p,
-            near_kv,
-            co_p,
-            norms,
-            outputs,
-            gsecond,
-            gnorm_e,
-        ) = forward(
-            lines,
-            pairs,
-            spans,
-            each,
-            live,
-            w_master,
-            small,
-            inputs,
-            perm,
-            cotangent.reshape(count, dim),
-            near,
+        order = row_order.reshape(1, dim)
+        _, grads, outputs, grad_inputs, norm_grads = layer(
+            lines, pairs, spans, each, live, w_master, small, inputs, order, cot, near
         )
+        grad_shard, norm_sums = reduce_grads(lines, grads, norm_grads)
+        norm_shard = lax.dynamic_slice(norm_sums, (0, lax.axis_index("dp") * part), (6, part))
     else:
+        perm = (jnp.arange(dim)[:, None] == row_order[None, :]).astype(bf16)
+        perm_att = jnp.pad(perm.reshape(shares, held * HEAD, dim), ((0, 0), (0, spare), (0, 0)))
+        perm_att = perm_att.reshape(shares * width, dim)
         weights = lax.all_gather(w_master.astype(bf16), "dp", axis=0, tiled=True)
         weights = lax.all_gather(weights, "seq", axis=1, tiled=True)
         norms = lax.all_gather(n_master.astype(bf16), "dp", axis=1, tiled=True).astype(f32)
@@ -1810,51 +1686,25 @@
         att_p, first, hid_p, cross_q, near_p, near_kv, co_p, second = cross_forward(
             spans, each, live, att_tok, x, norms, perm, perm_att, near, weights
         )
-        outputs, gsecond, grads, gnorm_e = feed(
-            second, cotangent.reshape(count, dim), norms, perm, weights
-        )
-    gfirst, gatt_tok, grads, gnorm_c = cross_backward(
-        spans,
-        each,
-        lines if planar else 0,
-        live,
-        gsecond,
-        first,
-        norms,
-        perm,
-        perm_att,
-        att_p,
-        hid_p,
-        cross_q,
-        near_p,
-        near_kv,
-        co_p,
-        weights,
-        grads,
-    )
-    if planar:
-        others = jnp.concatenate(
-            [jnp.zeros((2, dim), f32), gnorm_c, gnorm_e, jnp.zeros((2, dim), f32)], axis=0
-        )
-        grads, grad_inputs, norm_grads = finish(
-            pairs,
-            lines,
-            qkv,
-            att,
-            gatt_tok,
-            lse,
-            hid,
-            x,
-            gfirst,
+        outputs, gsecond, grads, gnorm_e = feed(second, cot, norms, perm, weights)
+        gfirst, gatt_tok, grads, gnorm_c = cross_backward(
+            spans,
+            each,
+            live,
+            gsecond,
+            first,
             norms,
             perm,
-            others,
+            perm_att,
+            att_p,
+            hid_p,
+            cross_q,
+            near_p,
+            near_kv,
+            co_p,
             weights,
             grads,
         )
-        grad_shard, norm_sums = reduce_grads(lines, grads, norm_grads)
-        norm_shard = lax.dynamic_slice(norm_sums, (0, lax.axis_index("dp") * part), (6, part))
-    else:
         gatt = lax.all_to_all(
             gatt_tok.reshape(seqs, tokens, shares, width)
             .transpose(0, 2, 1, 3)

time: 337 us -> 319 us (0.947)
  Pallas kernels: 319 us -> 302 us
    pallas_call x3 -> x1, Pallas kernels: 231 us -> 213 us  [layer(): pl.pallas_call(partial(layer_kernel, lines, pairs, spans, neighbours), ou...]
where the time goes in v1:
time: 319 us; the launch traced here: 316 us
  Pallas kernels  302 us (95%)
  other arithmetic  7.39 us (2%)
  local copies, waits for them, and re-layouts  6.11 us (2%)
    pallas_call x1, Pallas kernels, layer(): pl.pallas_call(partial(layer_kernel, lines, pairs, spans, neighbours), ou...  213 us
    pallas_call x1, Pallas kernels, reduce_grads(): pl.pallas_call(partial(reduce_kernel, lines), out_shape=(jax.ShapeDtypeSt...  88.3 us
    add x2, other arithmetic, adam_update(): average = ema_decay * average + (1.0 - ema_decay) * weight  6.69 us

profile of v1, /device:TPU:0, one launch (start us, length us, event | category | flops | bytes accessed | tf_op | source)
XLA Modules:
  0.0 316.2 jit_solution(6630031908608076487)
XLA Ops:
  0.6 0.7 convert_element_type.5
  1.3 0.6 pad.4.norm_ref
  1.9 0.8 copy.24
  2.7 0.6 reshape.38.presence_ref
  3.3 1.3 reshape.39.order_ref
  4.6 213.4 %layer.1 = (bf16[768,12288]{1,0:T(8,128)(2,1)}, bf16[768,12288]{1,0:T(8,128)(2,1)}, bf16[512,768]{1,0:T(8,128)(2,1)}, f32[512,768]{1,0:T(8,128)}, f32[8,768]{1,0:T(8,128)}) custom-call(s32[16]{0:T(128)} %reshape.38.presence_ref, f32[192,1536]{1,0:T(8,128)} %w_ref.1, bf16[16,256]{1,0:T(8,128)(2,1)} %pad.4.norm_ref, bf16[4,128,768]{2,1,0:T(8,128)(2,1)} %x_ref.1, ...), custom_call_target="tpu_custom_call" | custom-call | tf_op jit(solution)/shard_map/layer/pallas_call | solution.py:1342
  218.0 0.0 copy-start.3
  218.0 0.0 copy-start.4
  218.0 0.0 copy-start.5
  218.0 0.0 copy-start.6
  218.0 0.0 copy-start
  218.1 88.3 %reduce_grads.1 = (f32[192,1536]{1,0:T(8,128)}, f32[8,768]{1,0:T(8,128)}) custom-call(bf16[768,12288]{1,0:T(8,128)(2,1)} %get-tuple-element.18.grads_ref, f32[8,768]{1,0:T(8,128)} %get-tuple-element.19.small_ref), custom_call_target="tpu_custom_call" | custom-call | tf_op jit(solution)/shard_map/reduce_grads/pallas_call | solution.py:1572
  306.3 0.0 copy-done.3
  306.4 0.0 copy-done.4
  306.4 0.0 copy-done.5
  306.4 0.0 copy-done.6
  306.4 1.4 add_multiply_fusion.1
  307.8 0.0 copy-done
  307.8 0.0 copy-start.2
  307.8 5.3 %add_multiply_fusion = (f32[192,1536]{1,0:T(8,128)}, f32[192,1536]{1,0:T(8,128)}, f32[192,1536]{1,0:T(8,128)}, f32[192,1536]{1,0:T(8,128)}) fusion(f32[192,1536]{1,0:T(8,128)} %param.21, f32[192,1536]{1,0:T(8,128)S(1)} %copy-done, f32[192,1536]{1,0:T(8,128)} %get-tuple-element.20, f32[192,1536]{1,0:T(8,128)} %param.20, f32[192,1536]{1,0:T(8,128)} %param.19), kind=kLoop, calls=%fused_computation.2 | loop fusion | flops 5013504 | bytes 10616832 | tf_op jit(solution)/shard_map/add | solution.py:1618
  313.1 0.0 copy-start.1
  313.1 0.0 copy-done.2
  313.1 0.9 copy.27
  314.0 0.8 copy-done.1
  314.8 1.1 copy.28
Async XLA Ops:
  218.0 88.3 %copy-start.3 = (f32[6,192]{1,0:T(8,128)S(1)}, f32[6,192]{1,0:T(8,128)}, u32[]{:S(2)}) copy-start(f32[6,192]{1,0:T(8,128)} %param.22) | copy-start | bytes 13828
  218.0 88.3 %copy-start.4 = (f32[6,192]{1,0:T(8,128)S(1)}, f32[6,192]{1,0:T(8,128)}, u32[]{:S(2)}) copy-start(f32[6,192]{1,0:T(8,128)} %param.25) | copy-start | bytes 13828
  218.0 88.3 %copy-start.5 = (f32[6,192]{1,0:T(8,128)S(1)}, f32[6,192]{1,0:T(8,128)}, u32[]{:S(2)}) copy-start(f32[6,192]{1,0:T(8,128)} %param.24) | copy-start | bytes 13828
  218.0 88.3 %copy-start.6 = (f32[6,192]{1,0:T(8,128)S(1)}, f32[6,192]{1,0:T(8,128)}, u32[]{:S(2)}) copy-start(f32[6,192]{1,0:T(8,128)} %param.23) | copy-start | bytes 13828
  218.0 89.8 %copy-start = (f32[192,1536]{1,0:T(8,128)S(1)}, f32[192,1536]{1,0:T(8,128)}, u32[]{:S(2)}) copy-start(f32[192,1536]{1,0:T(8,128)} %w_ref.1) | copy-start | bytes 3538948
  307.8 5.3 %copy-start.2 = (bf16[512,768]{1,0:T(8,128)(2,1)S(1)}, bf16[512,768]{1,0:T(8,128)(2,1)}, u32[]{:S(2)}) copy-start(bf16[512,768]{1,0:T(8,128)(2,1)} %get-tuple-element.16) | copy-start | bytes 2359300
  313.1 1.7 copy-start.1
